TPU v7x, 32 devices: a whole 2x2x4 slice. The times are simulated.
32 devices in a mesh: dp: 8 (over z, x), tensor: 4 (over y, core).
Axes of the slice: x: 2, y: 2, z: 4, core: 2. Of those that a mesh axis runs over, the one named last changes fastest.
Arguments:
- tokens: bfloat16 [4096, 768], P(('dp', 'tensor')), may hold values from -6 to 6
- cotangent: bfloat16 [4096, 768], P(('dp', 'tensor')), may hold values from -6 to 6
- w_qkv: bfloat16 [768, 3, 768], P('dp', None, 'tensor'), may hold values from -0.21875 to 0.21875
- w_out_attn: bfloat16 [768, 768], P('dp', 'tensor'), may hold values from -3 to 3
- w_router: bfloat16 [768, 4], P('dp'), may hold values from -0.109375 to 0.109375
- w_in: bfloat16 [768, 4, 3072], P('dp', None, 'tensor'), may hold values from -0.21875 to 0.21875
- w_out: bfloat16 [768, 4, 3072], P('dp', None, 'tensor'), may hold values from -0.875 to 0.875
- norm1_gain: bfloat16 [768], P('dp'), may hold values from 0.099609375 to 1.8984375
- norm2_gain: bfloat16 [768], P('dp'), may hold values from 0.099609375 to 1.8984375
- bias_table: bfloat16 [384], P('dp'), may hold values from -4 to 4
- seq_length: int32 [8], P('dp'), may hold values from 385 to 512, as said below
- expert_ids: int32 [4096], P('dp'), may hold values from 0 to 3
- expert_slots: int32 [4096], P('dp'), may hold values from -1 to 127, as said below
- buckets: int32 [1023], replicated, may hold values from 0 to 31
Outputs:
- layer_out: bfloat16 [4096, 768], P(('dp', 'tensor'))
- grad_tokens: float32 [4096, 768], P(('dp', 'tensor'))
- grad_w_qkv: float32 [768, 3, 768], P('dp', None, 'tensor')
- grad_w_out_attn: float32 [768, 768], P('dp', 'tensor')
- grad_w_router: float32 [768, 4], P('dp')
- grad_w_in: float32 [768, 4, 3072], P('dp', None, 'tensor')
- grad_w_out: float32 [768, 4, 3072], P('dp', None, 'tensor')
- grad_norm1_gain: float32 [768], P('dp')
- grad_norm2_gain: float32 [768], P('dp')
- grad_bias_table: float32 [384], P('dp')
Inputs may be any that keep to these rules, and one draw needn't show every extreme that they name: Positions at or past a group's seq_length are padding; some group is full. `expert_slots`: within one group no two tokens share an expert and a slot; -1 marks a token that is not sent (padding, or over the capacity of 128); in every group some expert's 128 slots are all used.
All inputs are finite; a program needn't handle non-finite values.
Results may differ from a plain program's by a relative error of at most 0.017.
Values may be sent and summed in bfloat16 or wider, within the bound.
No kernel may reach another device: no remote copies, remote signals or barrier semaphores. Data moves between devices by JAX's collectives and lax.ppermute only.
A program may use at most 192 MiB of HBM per device.

v0:
```python
import jax
import jax.numpy as jnp
from jax import lax
from jax.sharding import PartitionSpec as P

D = 768
H = 12
HD = 64
NB = 32
E = 4
SEQ = 512
CAP = 128


EPSILON = 1e-06
HIGHEST_PRECISION = lax.Precision.HIGHEST


def in_blocks(shard, dim, length):
    before, after = (shard.shape[:dim], shard.shape[dim + 1 :])
    return jnp.moveaxis(shard.reshape(*before, length, -1, *after), dim, 0)


def summed_on_arrival(shard, axis, dim):
    pieces = in_blocks(shard, dim, lax.axis_size(axis))
    arrived = lax.all_to_all(pieces, axis, split_axis=0, concat_axis=0, tiled=True)
    return arrived.astype(jnp.float32).sum(axis=0)


def side_by_side(arrays, axis, dim, along):
    columns = [a.reshape(*a.shape[:along], -1) for a in arrays]
    both = jnp.concatenate(columns, axis=along)
    out, at, done = (summed_on_arrival(both, axis, dim), 0, [])
    for a, column in zip(arrays, columns):
        section = out[..., at : at + column.shape[along]]
        done.append(section.reshape(*section.shape[:along], *a.shape[along:]))
        at += column.shape[along]
    return tuple(done)


def normalize(values, scale_gain):
    return (
        values * lax.rsqrt(jnp.mean(values * values, axis=-1, keepdims=True) + EPSILON) * scale_gain
    )


def expand_bias(relative, row_count, key_count):
    reverse = relative[:, ::-1]
    rolled = jnp.roll(reverse, -(row_count - 1), axis=1)
    period = key_count + row_count - 2
    tiled = jnp.tile(rolled, (1, row_count))[:, : row_count * period]
    return tiled.reshape(relative.shape[0], row_count, period)[:, :, :key_count]


def contract_rows(weight, left_rows):
    return jnp.einsum(
        "ecd,def->ecf",
        left_rows,
        lax.all_gather(weight, "dp", axis=0, tiled=True),
        preferred_element_type=jnp.float32,
    )


def expand_columns(weight, right_rows):
    return jnp.einsum(
        "ecf,def->ecd",
        right_rows,
        lax.all_gather(weight, "dp", axis=0, tiled=True),
        preferred_element_type=jnp.float32,
    )


def body(
    tokens,
    cotangent,
    w_qkv,
    w_out_attn,
    w_router,
    w_in,
    w_out,
    norm1_gain,
    norm2_gain,
    bias_table,
    seq_length,
    expert_ids,
    expert_slots,
    buckets,
):
    tensor_rank = lax.axis_index("tensor")
    local_rows = tokens.shape[0]
    local_width = w_qkv.shape[2]
    local_heads = local_width // HD
    first_row = tensor_rank * local_rows
    qkv_weight, attn_weight, gain_one, gain_two, router_weight, table_flat = (
        lax.all_gather(w_qkv, "dp", axis=0, tiled=True),
        lax.all_gather(w_out_attn, "dp", axis=0, tiled=True),
        lax.all_gather(norm1_gain, "dp", axis=0, tiled=True),
        lax.all_gather(norm2_gain, "dp", axis=0, tiled=True),
        lax.all_gather(w_router, "dp", axis=0, tiled=True),
        lax.all_gather(bias_table, "dp", axis=0, tiled=True),
    )
    gain_one = gain_one.astype(jnp.float32)
    gain_two = gain_two.astype(jnp.float32)
    inputs = tokens.astype(jnp.float32)
    normed_one = normalize(inputs, gain_one).astype(jnp.bfloat16)
    normed_all = lax.all_gather(normed_one, "tensor", axis=0, tiled=True)
    qkv_all = jnp.einsum(
        "td,dcf->tcf", normed_all, qkv_weight, preferred_element_type=jnp.float32
    ).astype(jnp.bfloat16)
    queries = qkv_all[:, 0].reshape(SEQ, local_heads, HD)
    keys_all = qkv_all[:, 1].reshape(SEQ, local_heads, HD)
    values_all = qkv_all[:, 2].reshape(SEQ, local_heads, HD)
    table_rows = lax.dynamic_slice_in_dim(
        table_flat.astype(jnp.float32).reshape(H, NB), tensor_rank * local_heads, local_heads, 0
    )
    bucket_table = (buckets[None, :] == jnp.arange(NB, dtype=jnp.int32)[:, None]).astype(
        jnp.float32
    )
    relative = jnp.dot(table_rows, bucket_table, precision=HIGHEST_PRECISION)
    key_live = jnp.arange(SEQ, dtype=jnp.int32) < seq_length[0]
    block_rows = min(512, SEQ)
    block_starts = jnp.arange(SEQ // block_rows, dtype=jnp.int32) * block_rows

    def scores_for():
        scores = (
            jnp.einsum("qhe,khe->hqk", queries, keys_all, preferred_element_type=jnp.float32)
            * 0.125
        )
        scores = scores + expand_bias(relative, block_rows, SEQ)
        return (queries, jnp.where(key_live[None, None, :], scores, -1e30))

    def forward_block(offset):
        query_block, scores = scores_for()
        highest = jnp.max(scores, axis=-1, keepdims=True)
        exponent = jnp.exp(scores - highest)
        totals = jnp.sum(exponent, axis=-1, keepdims=True)
        attn_probs = (exponent / totals).astype(jnp.bfloat16)
        output = jnp.einsum(
            "hqk,khe->qhe", attn_probs, values_all, preferred_element_type=jnp.float32
        ).astype(jnp.bfloat16)
        return (output, (highest + jnp.log(totals))[:, :, 0])

    head_blocks, lse_blocks = lax.map(forward_block, block_starts)
    heads_all = head_blocks.reshape(SEQ, local_width)
    part_rows = heads_all
    attended = lax.psum_scatter(
        lax.dot_general(
            part_rows, attn_weight, (((1,), (1,)), ((), ())), preferred_element_type=jnp.float32
        ),
        "tensor",
        scatter_dimension=0,
        tiled=True,
    )
    middle = inputs + attended
    normed_two = normalize(middle, gain_two).astype(jnp.bfloat16)
    normed_both, cotangent_all = (
        lax.all_gather(normed_two, "tensor", axis=0, tiled=True),
        lax.all_gather(cotangent, "tensor", axis=0, tiled=True),
    )
    logits_all = jnp.dot(normed_both, router_weight, preferred_element_type=jnp.float32)
    route_all = jax.nn.softmax(logits_all, axis=-1)
    chosen_mask = expert_ids[:, None] == jnp.arange(E, dtype=jnp.int32)[None, :]
    gate_all = jnp.sum(jnp.where(chosen_mask, route_all, 0.0), axis=-1)
    dispatched = expert_slots >= 0
    flat_slot = jnp.where(dispatched, expert_ids * CAP + expert_slots, E * CAP)
    owners = (
        jnp.zeros((E * CAP + 1,), jnp.int32)
        .at[flat_slot]
        .set(jnp.arange(SEQ, dtype=jnp.int32))[: E * CAP]
    )
    filled = jnp.zeros((E * CAP + 1,), jnp.bool_).at[flat_slot].set(True)[: E * CAP]
    clipped = jnp.minimum(flat_slot, E * CAP - 1)
    buffer = jnp.where(filled[:, None], normed_both[owners], 0).reshape(E, CAP, D)
    pre_act = contract_rows(w_in, buffer)
    activation = jax.nn.gelu(pre_act).astype(jnp.bfloat16)
    expert_out = expand_columns(w_out, activation)
    expert_flat = expert_out.reshape(E * CAP, D)
    slot_index = clipped
    keep_mask = dispatched
    combined = lax.psum_scatter(
        jnp.where(keep_mask[:, None], expert_flat[slot_index], 0.0).astype(jnp.bfloat16),
        "tensor",
        scatter_dimension=0,
        tiled=True,
    ).astype(jnp.float32)
    gate_local = lax.dynamic_slice_in_dim(gate_all, first_row, local_rows, 0)
    layer_out = (middle + gate_local[:, None] * combined).astype(jnp.bfloat16)
    grad_output = cotangent.astype(jnp.float32)
    grad_gate = jnp.sum(grad_output * combined, axis=-1)
    grad_combined = (gate_all[:, None] * cotangent_all.astype(jnp.float32)).astype(jnp.bfloat16)
    grad_expert = jnp.where(filled[:, None], grad_combined[owners], 0).reshape(E, CAP, D)
    grad_act = contract_rows(w_out, grad_expert)
    _, gelu_pull = jax.vjp(jax.nn.gelu, pre_act)
    grad_pre = gelu_pull(grad_act)[0].astype(jnp.bfloat16)
    grad_buffer = expand_columns(w_in, grad_pre)
    grad_buffer_flat = grad_buffer.reshape(E * CAP, D)
    slot_index = clipped
    keep_mask = dispatched
    grad_normed_two = lax.psum_scatter(
        jnp.where(keep_mask[:, None], grad_buffer_flat[slot_index], 0.0).astype(jnp.bfloat16),
        "tensor",
        scatter_dimension=0,
        tiled=True,
    ).astype(jnp.float32)
    expert_grads = lax.psum_scatter(
        jnp.stack(
            [
                jnp.einsum("ecd,ecf->def", buffer, grad_pre, preferred_element_type=jnp.float32),
                jnp.einsum(
                    "ecd,ecf->def", grad_expert, activation, preferred_element_type=jnp.float32
                ),
            ],
            axis=1,
        ),
        "dp",
        scatter_dimension=0,
        tiled=True,
    )
    summed_in_grad = expert_grads[:, 0]
    summed_out_grad = expert_grads[:, 1]
    route_local = lax.dynamic_slice_in_dim(route_all, first_row, local_rows, 0)
    mask_local = lax.dynamic_slice_in_dim(chosen_mask, first_row, local_rows, 0).astype(jnp.float32)
    grad_logits = gate_local[:, None] * (mask_local - route_local) * grad_gate[:, None]
    grad_router = jnp.dot(
        normed_two.astype(jnp.float32).T, grad_logits, precision=HIGHEST_PRECISION
    )
    grad_normed_two = grad_normed_two + jnp.dot(
        grad_logits, router_weight.astype(jnp.float32).T, precision=HIGHEST_PRECISION
    )
    _, norm_pull_two = jax.vjp(normalize, middle, gain_two)
    grad_mid_norm, grad_gain_two = norm_pull_two(grad_normed_two)
    grad_middle = grad_output + grad_mid_norm
    grad_attended = grad_middle.astype(jnp.bfloat16)
    grad_att_all = lax.all_gather(grad_attended, "tensor", axis=0, tiled=True)
    grad_attn_weight = lax.dot_general(
        grad_att_all, heads_all, (((0,), (0,)), ((), ())), preferred_element_type=jnp.float32
    )
    grad_heads = jnp.dot(grad_att_all, attn_weight, preferred_element_type=jnp.float32).astype(
        jnp.bfloat16
    )
    grad_heads = grad_heads.reshape(SEQ, local_heads, HD)

    def backward_block(carried, block_item):
        grad_keys, grad_values, grad_relative = carried
        offset, lse_block = block_item
        query_block, scores = scores_for()
        probs_full = jnp.exp(scores - lse_block[:, :, None])
        grad_values = grad_values + jnp.einsum(
            "hqk,qhe->khe",
            probs_full.astype(jnp.bfloat16),
            grad_heads,
            preferred_element_type=jnp.float32,
        )
        grad_probs = jnp.einsum(
            "qhe,khe->hqk", grad_heads, values_all, preferred_element_type=jnp.float32
        )
        inner = jnp.sum(probs_full * grad_probs, axis=-1, keepdims=True)
        grad_scores = (probs_full * (grad_probs - inner)).astype(jnp.bfloat16)
        grad_query = (
            jnp.einsum("hqk,khe->qhe", grad_scores, keys_all, preferred_element_type=jnp.float32)
            * 0.125
        )
        grad_keys = (
            grad_keys
            + jnp.einsum(
                "hqk,qhe->khe", grad_scores, query_block, preferred_element_type=jnp.float32
            )
            * 0.125
        )
        _, bias_pull = jax.vjp(lambda relation: expand_bias(relation, block_rows, SEQ), relative)
        grad_relative = grad_relative + bias_pull(grad_scores.astype(jnp.float32))[0]
        return ((grad_keys, grad_values, grad_relative), grad_query)

    zero_keys = jnp.zeros((SEQ, local_heads, HD), jnp.float32)
    initial = (zero_keys, zero_keys, jnp.zeros_like(relative))
    (grad_keys, grad_values, grad_relative), grad_queries = lax.scan(
        backward_block, initial, (block_starts, lse_blocks)
    )
    grad_qkv = jnp.stack(
        [
            grad_queries.reshape(SEQ, local_width),
            grad_keys.reshape(SEQ, local_width),
            grad_values.reshape(SEQ, local_width),
        ],
        axis=1,
    ).astype(jnp.bfloat16)
    grad_qkv_weight = jnp.einsum(
        "td,tcf->dcf", normed_all, grad_qkv, preferred_element_type=jnp.float32
    )
    part_rows = grad_qkv
    grad_normed_one = lax.psum_scatter(
        jnp.einsum("tcf,dcf->td", part_rows, qkv_weight, preferred_element_type=jnp.float32).astype(
            jnp.bfloat16
        ),
        "tensor",
        scatter_dimension=0,
        tiled=True,
    ).astype(jnp.float32)
    _, norm_pull_one = jax.vjp(normalize, inputs, gain_one)
    grad_input_norm, grad_gain_one = norm_pull_one(grad_normed_one)
    grad_tokens = grad_middle + grad_input_norm
    grad_table_rows = jnp.dot(grad_relative, bucket_table.T, precision=HIGHEST_PRECISION)
    grad_table = lax.dynamic_update_slice_in_dim(
        jnp.zeros((H, NB), jnp.float32), grad_table_rows, tensor_rank * local_heads, 0
    ).reshape(H * NB)
    dp_sums = (
        *side_by_side(
            (
                grad_qkv_weight.astype(jnp.bfloat16),
                grad_attn_weight.astype(jnp.bfloat16),
                grad_gain_one.astype(jnp.bfloat16),
                grad_gain_two.astype(jnp.bfloat16),
                grad_router.astype(jnp.bfloat16),
            ),
            "dp",
            0,
            1,
        ),
        summed_on_arrival(grad_table.astype(jnp.bfloat16), "dp", 0),
    )
    tensor_sums = lax.psum((dp_sums[2], dp_sums[3], dp_sums[4], dp_sums[5]), "tensor")
    return (
        layer_out,
        grad_tokens,
        dp_sums[0],
        dp_sums[1],
        tensor_sums[2],
        summed_in_grad,
        summed_out_grad,
        tensor_sums[0],
        tensor_sums[1],
        tensor_sums[3],
    )


def solution(mesh):
    in_specs = (
        P(("dp", "tensor"), None),
        P(("dp", "tensor"), None),
        P("dp", None, "tensor"),
        P("dp", "tensor"),
        P("dp", None),
        P("dp", None, "tensor"),
        P("dp", None, "tensor"),
        P("dp"),
        P("dp"),
        P("dp"),
        P("dp"),
        P("dp"),
        P("dp"),
        P(),
    )
    out_specs = (
        P(("dp", "tensor"), None),
        P(("dp", "tensor"), None),
        P("dp", None, "tensor"),
        P("dp", "tensor"),
        P("dp", None),
        P("dp", None, "tensor"),
        P("dp", None, "tensor"),
        P("dp"),
        P("dp"),
        P("dp"),
    )
    return jax.shard_map(body, mesh=mesh, in_specs=in_specs, out_specs=out_specs, check_vma=False)
```

profile of v0, /device:TPU:0, one launch (start us, length us, event | category | flops | bytes accessed | tf_op | source)
XLA Modules:
  0.0 1061.3 jit_solution(5737888771705473886)
XLA Ops:
  13.3 23.9 %all-reduce.10 = (bf16[768]{0:T(1024)(128)(2,1)S(1)}, bf16[12,32]{1,0:T(8,128)(2,1)S(1)}, bf16[768]{0:T(1024)(128)(2,1)}) all-reduce(bf16[768]{0:T(1024)(128)(2,1)S(1)} %dynamic-update-slice, bf16[12,32]{1,0:T(8,128)(2,1)S(1)} %reshape.202, bf16[768]{0:T(1024)(128)(2,1)S(1)} %dynamic-update-slice.2), channel_id=1, replica_groups=mesh['dp'=8,'tensor'=4] {'dp'}, use_global_device_ids=true, to_apply=%add.4 | all-reduce | flops 1920 | bytes 7680
  39.1 35.3 %all_gather.40 = bf16[768,3,192]{2,1,0:T(4,128)(2,1)S(1)} all-gather(bf16[96,3,192]{2,1,0:T(4,128)(2,1)S(1)} %copy.111), channel_id=1, replica_groups=mesh['dp'=8,'tensor'=4] {'dp'}, dimensions={0}, use_global_device_ids=true | all-gather | bytes 995328 | tf_op jit(solution)/shard_map/all_gather | solution.py:95
  75.6 8.6 all_gather.39
  86.6 3.5 tile.24
  90.2 13.4 %tile.25 = f32[3,523776]{1,0:T(4,128)} reshape(f32[3,512,1023]{2,1,0:T(8,128)} %tile.24) | data formatting | bytes 12570624 | tf_op jit(solution)/shard_map/while/body/eval_jaxpr/tile | solution.py:51
  103.6 7.6 slice.99
  111.2 13.3 %reshape.203 = f32[3,512,1022]{2,1,0:T(8,128)} reshape(f32[3,523264]{1,0:T(4,128)} %slice.99) | data formatting | bytes 12558336 | tf_op jit(solution)/shard_map/while/body/eval_jaxpr/reshape | solution.py:52
  126.4 2.3 copy.137
  129.4 31.4 %all_gather.42 = bf16[768,192]{1,0:T(8,128)(2,1)S(1)} all-gather(bf16[96,192]{1,0:T(8,128)(2,1)} %param.17), channel_id=1, replica_groups=mesh['dp'=8,'tensor'=4] {'dp'}, dimensions={0}, use_global_device_ids=true | all-gather | bytes 331776 | tf_op jit(solution)/shard_map/all_gather | solution.py:96
  160.9 2.9 fusion.58
  167.7 2.0 copy.116
  171.9 19.4 %all-gather = bf16[8,96,4]{1,2,0:T(4,128)(2,1)S(1)} all-gather(bf16[1,96,4]{1,2,0:T(4,128)(2,1)S(1)} %bitcast.117), channel_id=1, replica_groups=mesh['dp'=8,'tensor'=4] {'dp'}, dimensions={0}, use_global_device_ids=true | all-gather | bytes 6912 | tf_op jit(solution)/shard_map/all_gather | solution.py:99
  191.9 2.4 scatter_custom_fusion.1
  194.4 2.9 scatter_custom_fusion
  199.0 7.9 all_gather.48
  209.4 9.2 all_gather.44
  218.6 4.3 gather_fusion
  226.3 2.2 multiply_convert_fusion.1
  228.5 4.5 gather_fusion.2
  232.9 15.8 %all-gather.4.cloned.1.call-done = bf16[768,4,768]{2,0,1:T(8,128)(2,1)} async-done(((bf16[96,4,768]{2,0,1:T(8,128)(2,1)}), bf16[768,4,768]{2,0,1:T(8,128)(2,1)}) %all-gather.4.cloned.1.call-update) | async-done | bytes 4718608 | tf_op jit(solution)/shard_map/all_gather | solution.py:59
  248.8 4.6 fusion.19
  253.4 75.4 %all-gather.6.cloned.1.call-done = bf16[768,4,768]{2,0,1:T(8,128)(2,1)} async-done(((bf16[96,4,768]{2,0,1:T(8,128)(2,1)}), bf16[768,4,768]{2,0,1:T(8,128)(2,1)}) %all-gather.6.cloned.1.call-update) | async-done | bytes 4718608 | tf_op jit(solution)/shard_map/all_gather | solution.py:68
  328.9 4.8 fusion.8
  333.7 2.5 fusion.63
  336.3 4.3 gather_fusion.3
  340.6 5.4 fusion.54
  346.0 4.3 gather_fusion.1
  350.4 2.9 select_convert_fusion
  356.6 18.4 %reduce-scatter.7.cloned.1.call-done = bf16[128,768]{1,0:T(8,128)(2,1)} async-done(((bf16[512,768]{1,0:T(8,128)(2,1)}), bf16[128,768]{1,0:T(8,128)(2,1)}) %reduce-scatter.7.cloned.1.call-update) | async-done | bytes 196624 | tf_op jit(solution)/shard_map/reduce_scatter | solution.py:180
  376.6 24.2 %reduce-scatter.9.cloned.1.call-done = bf16[128,768]{1,0:T(8,128)(2,1)} async-done(((bf16[512,768]{1,0:T(8,128)(2,1)}), bf16[128,768]{1,0:T(8,128)(2,1)}) %reduce-scatter.9.cloned.1.call-update) | async-done | bytes 196624 | tf_op jit(solution)/shard_map/reduce_scatter | solution.py:199
  400.8 2.2 multiply_reduce_fusion.1
  404.9 8.2 all_gather.49
  420.7 2.7 convolution_bitcast_fusion.1
  424.9 6.9 pad_maximum_fusion
  431.8 22.7 %copy.126 = f32[768,2,4,768]{3,2,1,0:T(4,128)} copy(f32[768,2,4,768]{0,3,2,1:T(8,128)} %pad_maximum_fusion) | data formatting | bytes 37748736 | tf_op jit(solution)/shard_map/stack | solution.py:206
  459.3 7.8 reshape.300
  467.0 5.1 reshape.211
  472.2 6.8 pad_convert_fusion
  479.0 13.1 %reshape.215 = f32[3,512,1023]{2,1,0:T(8,128)} reshape(f32[3,523776]{1,0:T(4,128)} %pad_convert_fusion) | data formatting | bytes 12570624 | tf_op jit(solution)/shard_map/while/body/eval_jaxpr/transpose(jvp())/reshape | solution.py:51
  492.1 3.3 reduce_sum.165
  498.2 2.5 concatenate.18
  504.4 5.6 all-to-all-start.1
  514.9 3.6 copy.122
  518.5 6.1 all-to-all-start
  526.5 67.1 %all-to-all-done = bf16[8,96,774]{2,1,0:T(8,128)(2,1)S(1)} async-done(((bf16[8,96,774]{2,1,0:T(8,128)(2,1)}), bf16[8,96,774]{2,1,0:T(8,128)(2,1)S(1)}, u32[]{:S(2)}, u32[]{:S(2)}) %all-to-all-start) | async-done | bytes 1188896 | tf_op jit(solution)/shard_map/all_to_all | solution.py:26
  595.8 12.0 %all-reduce.9 = (f32[96,4]{1,0:T(8,128)S(1)}, f32[96]{0:T(128)}, f32[96]{0:T(128)}, f32[48]{0:T(128)}) all-reduce(f32[96,4]{1,0:T(8,128)S(1)} %slice.103, f32[96]{0:T(128)S(1)} %get-tuple-element.135, f32[96]{0:T(128)S(1)} %get-tuple-element.134, f32[48]{0:T(128)S(1)} %convert_reduce_fusion.1), channel_id=1, replica_groups=mesh['dp'=8,'tensor'=4] {'tensor'}, use_global_device_ids=true, to_apply=%region_20.21 | all-reduce | flops 624 | bytes 4992 | tf_op jit(solution)/shard_map/psum | solution.py:321
  608.4 441.7 %all-reduce.13.cloned.1.call-done = f32[768,2,4,768]{3,2,1,0:T(4,128)} async-done(((f32[768,2,4,768]{3,2,1,0:T(4,128)}), f32[768,2,4,768]{3,2,1,0:T(4,128)}) %all-reduce.13.cloned.1.call-update) | async-done | bytes 18874384
  1050.1 3.4 dynamic-slice_bitcast_fusion
  (255 shorter events, 61.2 us)
Async XLA Ops:
  8.0 198.8 %reduce-scatter.5.cloned.1.call-start = ((), (), s32[]{:S(2)}) async-start(), calls=%async_computation.6 | async-start | bytes 1966080 | tf_op jit(solution)/shard_map/reduce_scatter | solution.py:146
  38.1 37.2 %copy-start.42 = (f32[3,1023]{1,0:T(4,128)}, f32[3,1023]{1,0:T(4,128)S(1)}, u32[]{:S(2)}) copy-start(f32[3,1023]{1,0:T(4,128)S(1)} %fusion.36) | copy-start | bytes 36832
  75.3 9.6 copy-start.11
  75.4 8.8 copy-start.65
  75.5 8.8 copy-start.55
  85.8 75.0 %copy-start.23 = (bf16[512,1,192]{0,2,1:T(8,128)(2,1)}, bf16[512,1,192]{0,2,1:T(8,128)(2,1)S(1)}, u32[]{:S(2)}) copy-start(bf16[512,1,192]{0,2,1:T(8,128)(2,1)S(1)} %get-tuple-element.149) | copy-start | bytes 589828
  85.8 75.0 %copy-start.25 = (bf16[512,1,192]{0,2,1:T(8,128)(2,1)}, bf16[512,1,192]{0,2,1:T(8,128)(2,1)S(1)}, u32[]{:S(2)}) copy-start(bf16[512,1,192]{0,2,1:T(8,128)(2,1)S(1)} %get-tuple-element.150) | copy-start | bytes 589828
  160.9 4.5 copy-start.13
  167.6 4.2 copy-start.59
  167.6 4.2 copy-start.63
  167.6 24.2 %copy-start.45 = (s32[512]{0:T(512)S(1)}, s32[512]{0:T(512)}, u32[]{:S(2)}) copy-start(s32[512]{0:T(512)} %param.25) | copy-start | bytes 6148
  167.7 24.2 %copy-start.51 = (s32[512]{0:T(512)S(1)}, s32[512]{0:T(512)}, u32[]{:S(2)}) copy-start(s32[512]{0:T(512)} %param.26) | copy-start | bytes 6148
  167.7 31.3 %copy-start.19 = (bf16[128,768]{1,0:T(8,128)(2,1)S(1)}, bf16[128,768]{1,0:T(8,128)(2,1)}, u32[]{:S(2)}) copy-start(bf16[128,768]{1,0:T(8,128)(2,1)} %param.15) | copy-start | bytes 589828
  167.7 81.1 %all-gather.4.cloned.1.call-start = ((), (), s32[]{:S(2)}) async-start(), calls=%async_computation.7 | async-start | bytes 5308416 | tf_op jit(solution)/shard_map/all_gather | solution.py:59
  169.7 159.1 %all-gather.6.cloned.1.call-start = ((), (), s32[]{:S(2)}) async-start(), calls=%async_computation.8 | async-start | bytes 5308416 | tf_op jit(solution)/shard_map/all_gather | solution.py:68
  171.8 203.2 %reduce-scatter.7.cloned.1.call-start = ((), (), s32[]{:S(2)}) async-start(), calls=%async_computation.9 | async-start | bytes 983040 | tf_op jit(solution)/shard_map/reduce_scatter | solution.py:180
  197.3 21.3 %copy-start.48 = (s32[1024]{0:T(1024)}, s32[1024]{0:T(1024)S(1)}, u32[]{:S(2)}) copy-start(s32[1024]{0:T(1024)S(1)} %pad_clamp_fusion.1) | copy-start | bytes 12292
  208.6 10.0 copy-start.52
  228.5 20.3 %copy-start.43 = (pred[4,128]{1,0:T(4,128)(4,1)S(1)}, pred[4,128]{1,0:T(4,128)(4,1)}, u32[]{:S(2)}) copy-start(pred[4,128]{1,0:T(4,128)(4,1)} %slice_bitcast_fusion) | copy-start | bytes 1540
  328.9 4.8 copy-start
  346.0 4.3 copy-start.62
  350.4 3.7 copy-start.46
  353.3 47.6 %reduce-scatter.9.cloned.1.call-start = ((), (), s32[]{:S(2)}) async-start(), calls=%async_computation.10 | async-start | bytes 983040 | tf_op jit(solution)/shard_map/reduce_scatter | solution.py:199
  354.0 157.8 %reduce-scatter.11.cloned.1.call-start = ((), (), s32[]{:S(2)}) async-start(), calls=%async_computation.11 | async-start | bytes 983040 | tf_op jit(solution)/shard_map/reduce_scatter | solution.py:291
  400.8 13.1 %copy-start.14 = (bf16[768,192]{1,0:T(8,128)(2,1)S(1)}, bf16[768,192]{1,0:T(8,128)(2,1)}, u32[]{:S(2)}) copy-start(bf16[768,192]{1,0:T(8,128)(2,1)} %copy-done.13) | copy-start | bytes 884740
  415.3 3.2 copy-start.31
  420.6 2.8 copy-start.3
  420.6 2.8 copy-start.17
  420.6 629.5 %all-reduce.13.cloned.1.call-start = ((), (), s32[]{:S(2)}) async-start(), calls=%async_computation.12 | async-start | bytes 37748736
  492.1 3.3 copy-start.32
  492.1 3.3 copy-start.34
  492.1 3.3 copy-start.36
  498.1 3.3 copy-start.50
  498.1 3.4 copy-start.22
  498.1 3.4 copy-start.54
  498.1 3.4 copy-start.57
  503.5 8.3 copy-start.10
  503.5 8.3 copy-start.56
  504.4 14.1 %all-to-all-start.1 = ((bf16[8,1,48]{2,1,0:T(2,128)(2,1)}), bf16[8,1,48]{2,1,0:T(2,128)(2,1)S(1)}, u32[]{:S(2)}, u32[]{:S(2)}) async-start(bf16[8,1,48]{2,1,0:T(2,128)(2,1)} %convert_element_type.187), calls=%async_computation.5 | async-start | bytes 8192 | tf_op jit(solution)/shard_map/all_to_all | solution.py:26
  518.4 6.9 copy-start.66
  518.4 6.9 copy-start.16
  518.5 6.9 copy-start.20
  518.5 6.9 copy-start.37
  518.5 6.9 copy-start.38
  518.5 6.9 copy-start.53
  518.5 6.9 copy-start.58
  518.5 6.9 copy-start.61
  518.5 75.1 %all-to-all-start = ((bf16[8,96,774]{2,1,0:T(8,128)(2,1)}), bf16[8,96,774]{2,1,0:T(8,128)(2,1)S(1)}, u32[]{:S(2)}, u32[]{:S(2)}) async-start(bf16[8,96,774]{2,1,0:T(8,128)(2,1)} %copy.122), calls=%async_computation.4 | async-start | bytes 2752512 | tf_op jit(solution)/shard_map/all_to_all | solution.py:26
  (34 other events, 50.5 us)
Sparse Core Ops, SparseCore 0:
  167.7 26.8 reduce-scatter.4
  353.4 21.5 reduce-scatter.6
  377.5 23.2 reduce-scatter.8
  420.7 23.6 reduce-scatter.10
Sparse Core Ops, SparseCore 1:
  170.6 78.1 all-gather.3
  251.1 77.7 all-gather.5
  454.6 595.5 all-reduce.12
where the time goes:
time: 1070 us; the launch traced here: 1060 us
  waiting for transfers between devices  643 us (60%)
  local copies, waits for them, and re-layouts  157 us (15%)
  blocking collectives  156 us (15%)
  matrix products  38.3 us (4%)
  other arithmetic  35.7 us (3%)
  between operations  19.4 us (2%)
  starting transfers between devices  12.2 us (1%)
    unnamed x8, waiting for transfers between devices  442 us
    all_gather x1, waiting for transfers between devices, expand_columns(): lax.all_gather(weight, 'dp', axis=0, tiled=True)  75.4 us
    all_to_all x2, waiting for transfers between devices, summed_on_arrival(): lax.all_to_all(pieces, axis, split_axis=0, concat_axis=0, tiled=True)  67.1 us
    all_gather x1, blocking collectives, body(): lax.all_gather(w_qkv, 'dp', axis=0, tiled=True)  35.3 us
    unnamed x159, local copies, waits for them, and re-layouts  34.6 us
    all_gather x1, blocking collectives, body(): lax.all_gather(w_out_attn, 'dp', axis=0, tiled=True)  31.4 us
    reduce_scatter x1, waiting for transfers between devices, body(): lax.psum_scatter(jnp.where(keep_mask[:, None], grad_buffer_flat[slot_inde...  24.2 us
    unnamed x1, blocking collectives  23.9 us
  transfers between devices with their start and end apart: 9, of which 6 were waited for; matrix products, arithmetic and copies ran while one was open for 12% of the time, Pallas kernels for 0%

commit v1 on v0

v1 whole, which is shorter than its diff:
```python
import functools

import jax
import jax.numpy as jnp
from jax import lax
from jax.experimental import pallas as pl
from jax.experimental.pallas import tpu as pltpu
from jax.sharding import PartitionSpec as P

D = 768
H = 12
HD = 64
NB = 32
E = 4
SEQ = 512
CAP = 128
T = 4
LH = H // T
LW = LH * HD
ROWS = SEQ // T
SUB = CAP // T
SPAN = 2 * SEQ
TILE = 128
TILES = SEQ // TILE

EPSILON = 1e-06
HIGHEST_PRECISION = lax.Precision.HIGHEST
BF = jnp.bfloat16
F32 = jnp.float32


def mm(a, b, ca, cb):
    return lax.dot_general(a, b, (((ca,), (cb,)), ((), ())), preferred_element_type=F32)


def over_t(x, k):
    return lax.ppermute(x, "tensor", [(i, i ^ k) for i in range(T)])


def over_z(x, d):
    n = lax.axis_size("dp")
    r = n // E
    return lax.ppermute(x, "dp", [(i, ((i // r) ^ d) * r + i % r) for i in range(n)])


def over_r(x, c):
    n = lax.axis_size("dp")
    r = n // E
    return lax.ppermute(x, "dp", [(i, (i // r) * r + ((i % r) ^ c)) for i in range(n)])


def natural(parts, index):
    bit = 1
    while bit < len(parts):
        flip = (index & bit) != 0
        parts = [jnp.where(flip, parts[j ^ bit], parts[j]) for j in range(len(parts))]
        bit *= 2
    return parts


def gather_t(x):
    far = over_t(x, 2)
    near, diagonal = over_t(x, 1), over_t(far, 1)
    return [x, near, far, diagonal]


def scatter_t(blocks):
    first = over_t(blocks[3], 1)
    second = over_t(blocks[1], 1)
    away = (blocks[2].astype(F32) + first.astype(F32)).astype(BF)
    home = blocks[0].astype(F32) + second.astype(F32)
    return home + over_t(away, 2).astype(F32)


def pick(x, index, axis):
    return lax.dynamic_index_in_dim(x, index, axis, keepdims=False)


def scatter_dp(x, z, r):
    n = x.shape[0]
    R = n // E
    x = x.reshape(E, R, *x.shape[1:])
    total = pick(x, r, 1).astype(F32)
    for c in range(1, R):
        total = total + over_r(pick(x, r ^ c, 1).astype(BF), c).astype(F32)
    low = total.astype(BF)
    out = pick(total, z, 0)
    for d in range(1, E):
        out = out + over_z(pick(low, z ^ d, 0), d).astype(F32)
    return out


def attention_forward(length, qkv_ref, rel_ref, probs_ref, heads_ref):
    live = lax.broadcasted_iota(jnp.int32, (TILE, SEQ), 1) < length[0]
    for h in range(LH):
        key = qkv_ref[:, LW + h * HD : LW + (h + 1) * HD]
        value = qkv_ref[:, 2 * LW + h * HD : 2 * LW + (h + 1) * HD]
        bias = jnp.broadcast_to(rel_ref[h : h + 1, :], (TILE, SPAN))
        for i in range(TILES):
            rows = slice(i * TILE, (i + 1) * TILE)
            query = qkv_ref[rows, h * HD : (h + 1) * HD]
            rolled = pltpu.roll(bias, SEQ + 1 + i * TILE, 1, stride=1, stride_axis=0)[:, :SEQ]
            scores = mm(query, key, 1, 1) * 0.125 + rolled
            scores = jnp.where(live, scores, -1e30)
            exponent = jnp.exp(scores - jnp.max(scores, axis=1, keepdims=True))
            probs = exponent / jnp.sum(exponent, axis=1, keepdims=True)
            probs_ref[h, rows, :] = probs
            heads_ref[rows, h * HD : (h + 1) * HD] = mm(probs.astype(BF), value, 1, 0).astype(BF)


def attention_backward(qkv_ref, probs_ref, grad_ref, out_ref, rel_ref):
    flip = (
        lax.broadcasted_iota(jnp.int32, (TILE, TILE), 0)
        + lax.broadcasted_iota(jnp.int32, (TILE, TILE), 1)
        == TILE - 1
    ).astype(BF)
    rel_ref[...] = jnp.zeros_like(rel_ref)
    for h in range(LH):
        key = qkv_ref[:, LW + h * HD : LW + (h + 1) * HD]
        value = qkv_ref[:, 2 * LW + h * HD : 2 * LW + (h + 1) * HD]
        grad_key = jnp.zeros((SEQ, HD), F32)
        grad_value = jnp.zeros((SEQ, HD), F32)
        diagonal = [None] * (2 * TILES - 1)
        for i in range(TILES):
            rows = slice(i * TILE, (i + 1) * TILE)
            query = qkv_ref[rows, h * HD : (h + 1) * HD]
            grad = grad_ref[rows, h * HD : (h + 1) * HD]
            probs = probs_ref[h, rows, :]
            grad_probs = mm(grad, value, 1, 1)
            inner = jnp.sum(probs * grad_probs, axis=1, keepdims=True)
            low = (probs * (grad_probs - inner)).astype(BF)
            out_ref[rows, h * HD : (h + 1) * HD] = (mm(low, key, 1, 0) * 0.125).astype(BF)
            grad_key = grad_key + mm(low, query, 0, 0)
            grad_value = grad_value + mm(probs.astype(BF), grad, 0, 0)
            for j in range(TILES):
                turned = mm(low[:, j * TILE : (j + 1) * TILE], flip, 1, 0)
                at = i - j + TILES - 1
                diagonal[at] = turned if diagonal[at] is None else diagonal[at] + turned
        out_ref[:, LW + h * HD : LW + (h + 1) * HD] = (grad_key * 0.125).astype(BF)
        out_ref[:, 2 * LW + h * HD : 2 * LW + (h + 1) * HD] = grad_value.astype(BF)
        for at, block in enumerate(diagonal):
            wide = jnp.concatenate([block, jnp.zeros((TILE, TILE), F32)], axis=1)
            line = jnp.sum(
                pltpu.roll(wide, 0, 1, stride=1, stride_axis=0), axis=0, keepdims=True
            )
            rel_ref[h : h + 1, at * TILE : (at + 2) * TILE] += line


VMEM = pl.BlockSpec(memory_space=pltpu.VMEM)
BIG = pltpu.CompilerParams(vmem_limit_bytes=40 * 2**20)


def attend(qkv, reversed_rel, length):
    return pl.pallas_call(
        attention_forward,
        out_shape=(
            jax.ShapeDtypeStruct((LH, SEQ, SEQ), F32),
            jax.ShapeDtypeStruct((SEQ, LW), BF),
        ),
        in_specs=[pl.BlockSpec(memory_space=pltpu.SMEM), VMEM, VMEM],
        out_specs=(VMEM, VMEM),
        compiler_params=BIG,
        cost_estimate=pl.CostEstimate(
            flops=4 * LH * SEQ * SEQ * HD,
            bytes_accessed=4 * LH * SEQ * SEQ,
            transcendentals=LH * SEQ * SEQ,
        ),
        name="attention_forward",
    )(length, qkv, reversed_rel)


def attend_back(qkv, probs, grad_heads):
    return pl.pallas_call(
        attention_backward,
        out_shape=(
            jax.ShapeDtypeStruct((SEQ, 3 * LW), BF),
            jax.ShapeDtypeStruct((LH, SPAN), F32),
        ),
        in_specs=[VMEM, VMEM, VMEM],
        out_specs=(VMEM, VMEM),
        compiler_params=BIG,
        cost_estimate=pl.CostEstimate(
            flops=12 * LH * SEQ * SEQ * HD, bytes_accessed=4 * LH * SEQ * SEQ, transcendentals=0
        ),
        name="attention_backward",
    )(qkv, probs, grad_heads)


def norm_scale(values):
    return lax.rsqrt(jnp.mean(values * values, axis=-1, keepdims=True) + EPSILON)


def norm_back(grad, values, scale, gain):
    u = grad * gain
    inner = jnp.mean(u * values, axis=-1, keepdims=True)
    return scale * u - scale * scale * scale * values * inner


def gather_weight(weight, z, r):
    parts = [pick(weight, z, 1)] + [over_z(pick(weight, z ^ d, 1), d) for d in range(1, E)]
    column = jnp.stack(natural(parts, z))
    n = lax.axis_size("dp")
    R = n // E
    every = [column] + [over_r(column, c) for c in range(1, R)]
    return jnp.stack(natural(every, r), axis=1).reshape(-1, weight.shape[2])


def scatter_weight(grad, z, r):
    n = lax.axis_size("dp")
    R = n // E
    x = grad.reshape(E, R, D // n, -1)
    total = pick(x, r, 1).astype(F32)
    for c in range(1, R):
        total = total + over_r(pick(x, r ^ c, 1).astype(BF), c).astype(F32)
    low = total.astype(BF)
    parts = [pick(low, z, 0)] + [over_z(pick(low, z ^ d, 0), d) for d in range(1, E)]
    return jnp.stack(natural(parts, z), axis=1).astype(F32)


def body(
    tokens,
    cotangent,
    w_qkv,
    w_out_attn,
    w_router,
    w_in,
    w_out,
    norm1_gain,
    norm2_gain,
    bias_table,
    seq_length,
    expert_ids,
    expert_slots,
    buckets,
):
    n = lax.axis_size("dp")
    R = n // E
    at_dp = lax.axis_index("dp")
    z, r = at_dp // R, at_dp % R
    t = lax.axis_index("tensor")
    local = D // n

    table_column = jnp.pad(bias_table, (0, local - bias_table.shape[0]))
    packed = jnp.concatenate(
        [
            w_qkv.reshape(local, 3 * LW),
            w_out_attn,
            w_router,
            norm1_gain[:, None],
            norm2_gain[:, None],
            table_column[:, None],
        ],
        axis=1,
    )
    packed = lax.all_gather(packed, "dp", axis=0, tiled=True)
    qkv_weight = packed[:, : 3 * LW]
    attn_weight = packed[:, 3 * LW : 4 * LW]
    router_weight = packed[:, 4 * LW : 4 * LW + E]
    gain_one = packed[:, 4 * LW + E].astype(F32)
    gain_two = packed[:, 4 * LW + E + 1].astype(F32)
    table_flat = packed[:, 4 * LW + E + 2].reshape(n, local)[:, : H * NB // n].reshape(-1)

    token_parts = gather_t(tokens)
    tokens_all = jnp.concatenate(natural(token_parts, t), axis=0)
    cotangent_all = jnp.concatenate(natural(gather_t(cotangent), t), axis=0)

    sent = expert_slots >= 0
    absolute = jnp.where(sent, expert_ids * CAP + expert_slots, -1)
    position = jnp.arange(SEQ, dtype=jnp.int32)
    empty = ~jnp.any(absolute[None, :] == position[:, None], axis=1)
    before = position[None, :] <= position[:, None]
    empty_rank = jnp.sum((before & empty[None, :]).astype(jnp.int32), axis=1)
    unsent_rank = jnp.sum((before & ~sent[None, :]).astype(jnp.int32), axis=1)
    match = empty[None, :] & (empty_rank[None, :] == unsent_rank[:, None])
    spare = jnp.sum(jnp.where(match, position[None, :], 0), axis=1)
    slot = jnp.where(sent, absolute, spare)
    in_expert = slot % CAP
    place = ((in_expert // SUB) ^ t) * ROWS + ((slot // CAP) ^ z) * SUB + in_expert % SUB
    to_slots_mask = place[None, :] == position[:, None]
    to_slots = to_slots_mask.astype(BF)
    own_mask = to_slots_mask[:ROWS]
    sent_own = jnp.any(own_mask & sent[None, :], axis=1)
    chosen_own = jnp.sum(jnp.where(own_mask, expert_ids[None, :], 0), axis=1)
    own_tokens = lax.dynamic_slice_in_dim(place, t * ROWS, ROWS, 0)
    from_slots_own = (own_tokens[:, None] == position[None, :]).astype(BF)

    def dispatch(rows):
        rows = jnp.where(sent_own[:, None], rows, 0).astype(BF)
        blocks = [rows[d * SUB : (d + 1) * SUB] for d in range(E)]
        arrived = [blocks[0]] + [over_z(blocks[d], d) for d in range(1, E)]
        return jnp.concatenate(gather_t(jnp.concatenate(arrived, axis=0)), axis=0)

    grad_output = mm(to_slots[:ROWS], cotangent_all, 1, 0)
    expert_cotangent = dispatch(grad_output)
    in_weight = gather_weight(w_in, z, r)
    out_weight = gather_weight(w_out, z, r)

    inputs_all = tokens_all.astype(F32)
    scale_all = norm_scale(inputs_all)
    normed_all = (inputs_all * scale_all * gain_one).astype(BF)
    qkv = mm(normed_all, qkv_weight, 1, 0).astype(BF)
    table_rows = lax.dynamic_slice_in_dim(table_flat.astype(F32).reshape(H, NB), t * LH, LH, 0)
    bucket_table = (buckets[None, :] == jnp.arange(NB, dtype=jnp.int32)[:, None]).astype(F32)
    reversed_rel = jnp.dot(
        table_rows,
        jnp.pad(bucket_table[:, ::-1], ((0, 0), (0, 1))),
        precision=HIGHEST_PRECISION,
    )
    probs, heads_all = attend(qkv, reversed_rel, seq_length)
    heads_slots = mm(to_slots, heads_all, 1, 0).astype(BF)
    part = mm(heads_slots, attn_weight, 1, 1).astype(BF).reshape(T, ROWS, D)
    attended = scatter_t([part[k] for k in range(T)])
    inputs = mm(to_slots[:ROWS], tokens_all, 1, 0)
    middle = inputs + attended
    scale_two = norm_scale(middle)
    normed_two = (middle * scale_two * gain_two).astype(BF)

    buffer = dispatch(normed_two)

    def route_of(rows):
        return jax.nn.softmax(mm(rows, router_weight, 1, 0), axis=-1)

    experts = jnp.arange(E, dtype=jnp.int32)[None, :]
    expert_gate = jnp.sum(jnp.where(experts == z, route_of(buffer), 0.0), axis=-1)
    grad_expert = (expert_gate[:, None] * expert_cotangent.astype(F32)).astype(BF)
    pre_act = mm(buffer, in_weight, 1, 0)
    activation, gelu_pull = jax.vjp(jax.nn.gelu, pre_act)
    activation = activation.astype(BF)
    grad_act = mm(grad_expert, out_weight, 1, 0)
    grad_pre = gelu_pull(grad_act)[0].astype(BF)
    expert_out = mm(activation, out_weight, 1, 1).astype(BF)
    grad_buffer = mm(grad_pre, in_weight, 1, 1).astype(BF)
    both = jnp.concatenate([expert_out, grad_buffer], axis=1).reshape(T, ROWS, 2 * D)
    mine = scatter_t([both[k] for k in range(T)]).astype(BF)
    blocks = [mine[d * SUB : (d + 1) * SUB] for d in range(E)]
    returned = jnp.concatenate(
        [blocks[0]] + [over_z(blocks[d], d) for d in range(1, E)], axis=0
    ).astype(F32)
    combined, grad_normed_two = returned[:, :D], returned[:, D:]

    summed_out_grad = scatter_weight(mm(grad_expert, activation, 0, 0), z, r)
    summed_in_grad = scatter_weight(mm(buffer, grad_pre, 0, 0), z, r)

    route = route_of(normed_two)
    chosen = experts == chosen_own[:, None]
    gate = jnp.sum(jnp.where(chosen, route, 0.0), axis=-1)
    layer_rows = (middle + gate[:, None] * combined).astype(BF)
    grad_gate = jnp.sum(grad_output * combined, axis=-1)
    grad_logits = gate[:, None] * (chosen.astype(F32) - route) * grad_gate[:, None]
    grad_router = jnp.dot(normed_two.astype(F32).T, grad_logits, precision=HIGHEST_PRECISION)
    grad_normed_two = grad_normed_two + jnp.dot(
        grad_logits, router_weight.astype(F32).T, precision=HIGHEST_PRECISION
    )
    grad_gain_two = jnp.sum(grad_normed_two * middle * scale_two, axis=0)
    grad_middle = (grad_output + norm_back(grad_normed_two, middle, scale_two, gain_two)).astype(BF)
    grad_slots = jnp.concatenate(gather_t(grad_middle), axis=0)
    layer_slots = jnp.concatenate(gather_t(layer_rows), axis=0)
    layer_out = mm(from_slots_own, layer_slots, 1, 0).astype(BF)

    grad_attended = mm(to_slots, grad_slots, 0, 0).astype(BF)
    grad_heads = mm(grad_attended, attn_weight, 1, 0).astype(BF)
    grad_attn_weight = mm(grad_attended, heads_all, 0, 0)
    grad_qkv, grad_rel = attend_back(qkv, probs, grad_heads)
    grad_normed_part = mm(grad_qkv, qkv_weight, 1, 1)
    grad_qkv_weight = mm(normed_all, grad_qkv, 0, 0)
    grad_gain_one = jnp.sum(grad_normed_part * inputs_all * scale_all, axis=0)
    part = natural(list(grad_normed_part.astype(BF).reshape(T, ROWS, D)), t)
    grad_normed_one = scatter_t(part)
    own_inputs = tokens.astype(F32)
    grad_tokens = mm(from_slots_own, grad_slots, 1, 0) + norm_back(
        grad_normed_one, own_inputs, norm_scale(own_inputs), gain_one
    )
    grad_table_rows = jnp.dot(
        grad_rel,
        jnp.pad(bucket_table, ((0, 0), (0, 1))).T,
        precision=HIGHEST_PRECISION,
    )
    grad_table = lax.dynamic_update_slice_in_dim(
        jnp.zeros((H, NB), F32), grad_table_rows, t * LH, 0
    ).reshape(n, H * NB // n)

    def with_tail(matrix, columns):
        tail = jnp.concatenate(columns, axis=1)
        width = matrix.shape[2]
        tail = jnp.pad(tail, ((0, 0), (0, -tail.shape[1] % width)))
        return jnp.concatenate([matrix, tail.reshape(n, -1, width)], axis=1)

    early = scatter_dp(
        with_tail(
            grad_attn_weight.reshape(n, local, LW),
            [grad_router.reshape(n, local * E), grad_gain_two.reshape(n, local)],
        ),
        z,
        r,
    )
    late = scatter_dp(
        with_tail(
            grad_qkv_weight.reshape(n, local, 3 * LW),
            [grad_gain_one.reshape(n, local), grad_table],
        ),
        z,
        r,
    )
    early_tail = early[local:].reshape(-1)[: local * (E + 1)]
    late_tail = late[local:].reshape(-1)[: local + H * NB // n]
    small = jnp.concatenate([early_tail, late_tail]).reshape(1, -1)
    small = small + over_t(small, 1)
    small = (small + over_t(small, 2))[0]
    return (
        layer_out,
        grad_tokens,
        late[:local].reshape(local, 3, LW),
        early[:local],
        small[: local * E].reshape(local, E),
        summed_in_grad,
        summed_out_grad,
        small[local * (E + 1) : local * (E + 2)],
        small[local * E : local * (E + 1)],
        small[local * (E + 2) :],
    )


def solution(mesh):
    in_specs = (
        P(("dp", "tensor"), None),
        P(("dp", "tensor"), None),
        P("dp", None, "tensor"),
        P("dp", "tensor"),
        P("dp", None),
        P("dp", None, "tensor"),
        P("dp", None, "tensor"),
        P("dp"),
        P("dp"),
        P("dp"),
        P("dp"),
        P("dp"),
        P("dp"),
        P(),
    )
    out_specs = (
        P(("dp", "tensor"), None),
        P(("dp", "tensor"), None),
        P("dp", None, "tensor"),
        P("dp", "tensor"),
        P("dp", None),
        P("dp", None, "tensor"),
        P("dp", None, "tensor"),
        P("dp"),
        P("dp"),
        P("dp"),
    )
    return jax.shard_map(body, mesh=mesh, in_specs=in_specs, out_specs=out_specs, check_vma=False)
```

time: 1070 us -> 282 us (0.26)
  waiting for transfers between devices: 643 us -> 106 us
  blocking collectives: 156 us -> 0 us
  local copies, waits for them, and re-layouts: 157 us -> 32.7 us
  starting transfers between devices: 12.2 us -> 63.7 us
  other arithmetic: 35.7 us -> 19 us
    unnamed x8 -> x1, waiting for transfers between devices: 442 us -> 0.02 us
    all_gather x7 -> x0, blocking collectives: 120 us -> none  [the longest x1 35.3 us: body(): lax.all_gather(w_qkv, 'dp', axis=0, tiled=True)]
    ppermute x0 -> x62, waiting for transfers between devices: none -> 106 us  [the longest x27 45.3 us: over_z(): lax.ppermute(x, 'dp', [(i, (i // r ^ d) * r + i % r) for i in range(n)])]
    all_gather x2 -> x1, waiting for transfers between devices: 91.3 us -> 0.01 us  [body(): packed = lax.all_gather(packed, 'dp', axis=0, tiled=True)]
    all_to_all x2 -> x0, waiting for transfers between devices: 67.1 us -> none  [summed_on_arrival(): lax.all_to_all(pieces, axis, split_axis=0, concat_axis=0, tiled=True)]
    ppermute x0 -> x62, starting transfers between devices: none -> 63.7 us  [the longest x27 45 us: over_z(): lax.ppermute(x, 'dp', [(i, (i // r ^ d) * r + i % r) for i in range(n)])]
    reduce_scatter x4 -> x0, waiting for transfers between devices: 42.6 us -> none  [the longest x1 24.2 us: body(): lax.psum_scatter(jnp.where(keep_mask[:, None], grad_buffer_flat[slot_inde...]
    another operation x3, local copies, waits for them, and re-layouts: 39.6 us -> 0.24 us  [the longest x2 0.16 us: gather_weight(): return jnp.stack(natural(every, r), axis=1).reshape(-1, weight.shape[2])]
  transfers between devices with their start and end apart: 9 -> 63, of which waited for: 6 -> 24; matrix products, arithmetic and copies ran while one was open for 12% -> 24% of each run, Pallas kernels for 0% -> 4%
where the time goes in v1:
time: 282 us; the launch traced here: 277 us
  waiting for transfers between devices  106 us (38%)
  starting transfers between devices  63.7 us (23%)
  local copies, waits for them, and re-layouts  32.7 us (12%)
  matrix products  28.8 us (10%)
  other arithmetic  19 us (7%)
  between operations  16.6 us (6%)
  Pallas kernels  10.3 us (4%)
    ppermute x27, waiting for transfers between devices, over_z(): lax.ppermute(x, 'dp', [(i, (i // r ^ d) * r + i % r) for i in range(n)])  45.3 us
    ppermute x27, starting transfers between devices, over_z(): lax.ppermute(x, 'dp', [(i, (i // r ^ d) * r + i % r) for i in range(n)])  45 us
    ppermute x6, waiting for transfers between devices, over_r(): lax.ppermute(x, 'dp', [(i, i // r * r + (i % r ^ c)) for i in range(n)])  42.4 us
    dot_general x19, matrix products, mm(): lax.dot_general(a, b, (((ca,), (cb,)), ((), ())), preferred_element_type=...  25.9 us
    ppermute x29, waiting for transfers between devices, over_t(): return lax.ppermute(x, 'tensor', [(i, i ^ k) for i in range(T)])  18.5 us
    unnamed x135, local copies, waits for them, and re-layouts  13.5 us
    ppermute x29, starting transfers between devices, over_t(): return lax.ppermute(x, 'tensor', [(i, i ^ k) for i in range(T)])  12.4 us
    ppermute x6, starting transfers between devices, over_r(): lax.ppermute(x, 'dp', [(i, i // r * r + (i % r ^ c)) for i in range(n)])  6.27 us
  transfers between devices with their start and end apart: 63, of which 24 were waited for; matrix products, arithmetic and copies ran while one was open for 24% of the time, Pallas kernels for 4%

profile of v1, /device:TPU:0, one launch (start us, length us, event | category | flops | bytes accessed | tf_op | source)
XLA Modules:
  0.0 277.3 jit_solution(5482004308861648564)
XLA Ops:
  7.2 3.0 %collective-permute-start = (bf16[128,768]{1,0:T(8,128)(2,1)}, bf16[128,768]{1,0:T(8,128)(2,1)}, u32[]{:S(2)}, u32[]{:S(2)}) collective-permute-start(bf16[128,768]{1,0:T(8,128)(2,1)} %param.14), channel_id=1, source_target_pairs={{0,2},{1,3},{2,0},{3,1},{4,6},{5,7},{6,4},{7,5},{8,10},{9,11},{10,... | collective-permute-start | bytes 589832 | tf_op jit(solution)/shard_map/ppermute | solution.py:37
  14.7 2.4 constant_dynamic-slice_fusion.4
  17.2 3.7 %collective-permute-start.16 = (bf16[96,768]{1,0:T(8,128)(2,1)S(1)}, bf16[96,768]{1,0:T(8,128)(2,1)S(1)}, u32[]{:S(2)}, u32[]{:S(2)}) collective-permute-start(bf16[96,768]{1,0:T(8,128)(2,1)S(1)} %bitcast.215), channel_id=1, source_target_pairs={{0,24},{4,28},{8,16},{12,20},{16,8},{20,12},{24,0},{28,4},{1,25},{... | collective-permute-start | bytes 442376 | tf_op jit(solution)/shard_map/ppermute | solution.py:43
  26.9 3.6 %collective-permute-start.12 = (bf16[96,768]{1,0:T(8,128)(2,1)S(1)}, bf16[96,768]{1,0:T(8,128)(2,1)S(1)}, u32[]{:S(2)}, u32[]{:S(2)}) collective-permute-start(bf16[96,768]{1,0:T(8,128)(2,1)S(1)} %bitcast.218), channel_id=1, source_target_pairs={{0,24},{4,28},{8,16},{12,20},{16,8},{20,12},{24,0},{28,4},{1,25},{... | collective-permute-start | bytes 442376 | tf_op jit(solution)/shard_map/ppermute | solution.py:43
  30.5 12.5 %collective-permute-done.17 = bf16[96,768]{1,0:T(8,128)(2,1)S(1)} collective-permute-done((bf16[96,768]{1,0:T(8,128)(2,1)S(1)}, bf16[96,768]{1,0:T(8,128)(2,1)S(1)}, u32[]{:S(2)}, u32[]{:S(2)}) %collective-permute-start.17) | collective-permute-done | bytes 147488 | tf_op jit(solution)/shard_map/ppermute | solution.py:43
  43.1 3.0 %collective-permute-start.14 = (bf16[96,768]{1,0:T(8,128)(2,1)S(1)}, bf16[96,768]{1,0:T(8,128)(2,1)S(1)}, u32[]{:S(2)}, u32[]{:S(2)}) collective-permute-start(bf16[96,768]{1,0:T(8,128)(2,1)S(1)} %bitcast.216), channel_id=1, source_target_pairs={{0,8},{4,12},{8,0},{12,4},{16,24},{20,28},{24,16},{28,20},{1,9},{5... | collective-permute-start | bytes 442376 | tf_op jit(solution)/shard_map/ppermute | solution.py:43
  47.5 8.3 %collective-permute-done.13 = bf16[96,768]{1,0:T(8,128)(2,1)S(1)} collective-permute-done((bf16[96,768]{1,0:T(8,128)(2,1)S(1)}, bf16[96,768]{1,0:T(8,128)(2,1)S(1)}, u32[]{:S(2)}, u32[]{:S(2)}) %collective-permute-start.13) | collective-permute-done | bytes 147488 | tf_op jit(solution)/shard_map/ppermute | solution.py:43
  55.8 1.5 collective-permute-start.19
  61.7 10.3 %collective-permute-done.19 = bf16[4,96,768]{2,1,0:T(8,128)(2,1)S(1)} collective-permute-done((bf16[4,96,768]{2,1,0:T(8,128)(2,1)S(1)}, bf16[4,96,768]{2,1,0:T(8,128)(2,1)S(1)}, u32[]{:S(2)}, u32[]{:S(2)}) %collective-permute-start.19) | collective-permute-done | bytes 589856 | tf_op jit(solution)/shard_map/ppermute | solution.py:49
  74.4 1.9 convert_reduce_fusion.2
  76.4 2.0 convolution_convert_fusion.4.qkv_ref
  78.6 4.5 %attention_forward.1 = (f32[3,512,512]{2,1,0:T(8,128)S(1)}, bf16[512,192]{1,0:T(8,128)(2,1)S(1)}) custom-call(s32[1]{0:T(128)S(6)} %copy.269.length, bf16[512,576]{1,0:T(8,128)(2,1)S(1)} %convolution_convert_fusion.4.qkv_ref, f32[3,1024]{1,0:T(4,128)S(1)} %fusion.73.rel_ref), custom_call_target="tpu_custom_call" | custom-call | flops 201326592 | bytes 3145728 | tf_op jit(solution)/shard_map/attention_forward/pallas_call | solution.py:154
  83.9 2.8 %convolution_convert_fusion.2 = bf16[512,768]{1,0:T(8,128)(2,1)} fusion(bf16[512,192]{1,0:T(8,128)(2,1)S(1)} %get-tuple-element.14, s32[512]{0:T(512)} %copy-done.43, bf16[768,775]{1,0:T(8,128)(2,1)} %all-gather.2.cloned.1.call-done), kind=kOutput, calls=%fused_computation.28 | convolution fusion | flops 252411904 | bytes 1378304 | tf_op jit(solution)/shard_map/dot_general | solution.py:33
  90.9 6.0 %collective-permute-done.5 = bf16[128,768]{1,0:T(8,128)(2,1)S(1)} collective-permute-done((bf16[128,768]{1,0:T(8,128)(2,1)S(1)}, bf16[128,768]{1,0:T(8,128)(2,1)S(1)}, u32[]{:S(2)}, u32[]{:S(2)}) %collective-permute-start.5) | collective-permute-done | bytes 196640 | tf_op jit(solution)/shard_map/ppermute | solution.py:37
  97.7 1.7 collective-permute-start.6
  99.3 3.9 %collective-permute-start.7 = (bf16[32,768]{1,0:T(8,128)(2,1)S(1)}, bf16[32,768]{1,0:T(8,128)(2,1)S(1)}, u32[]{:S(2)}, u32[]{:S(2)}) collective-permute-start(bf16[32,768]{1,0:T(8,128)(2,1)S(1)} %get-tuple-element.185), channel_id=1, source_target_pairs={{0,16},{4,20},{8,24},{12,28},{16,0},{20,4},{24,8},{28,12},{1,17},{... | collective-permute-start | bytes 147464 | tf_op jit(solution)/shard_map/ppermute | solution.py:43
  103.9 3.8 %collective-permute-start.24 = (bf16[32,768]{1,0:T(8,128)(2,1)S(1)}, bf16[32,768]{1,0:T(8,128)(2,1)S(1)}, u32[]{:S(2)}, u32[]{:S(2)}) collective-permute-start(bf16[32,768]{1,0:T(8,128)(2,1)S(1)} %get-tuple-element.180), channel_id=1, source_target_pairs={{0,16},{4,20},{8,24},{12,28},{16,0},{20,4},{24,8},{28,12},{1,17},{... | collective-permute-start | bytes 147464 | tf_op jit(solution)/shard_map/ppermute | solution.py:43
  110.9 4.1 %collective-permute-done.25 = bf16[32,768]{1,0:T(8,128)(2,1)S(1)} collective-permute-done((bf16[32,768]{1,0:T(8,128)(2,1)S(1)}, bf16[32,768]{1,0:T(8,128)(2,1)S(1)}, u32[]{:S(2)}, u32[]{:S(2)}) %collective-permute-start.25) | collective-permute-done | bytes 49184 | tf_op jit(solution)/shard_map/ppermute | solution.py:43
  116.6 5.8 %collective-permute-done.27 = bf16[128,768]{1,0:T(8,128)(2,1)S(1)} collective-permute-done((bf16[128,768]{1,0:T(8,128)(2,1)S(1)}, bf16[128,768]{1,0:T(8,128)(2,1)S(1)}, u32[]{:S(2)}, u32[]{:S(2)}) %collective-permute-start.27) | collective-permute-done | bytes 196640 | tf_op jit(solution)/shard_map/ppermute | solution.py:37
  125.8 1.7 fusion.6
  129.9 1.5 collective-permute-start.54
  133.7 12.4 %collective-permute-done.54 = bf16[4,96,768]{2,1,0:T(8,128)(2,1)S(1)} collective-permute-done((bf16[4,96,768]{2,1,0:T(8,128)(2,1)S(1)}, bf16[4,96,768]{2,1,0:T(8,128)(2,1)S(1)}, u32[]{:S(2)}, u32[]{:S(2)}) %collective-permute-start.54) | collective-permute-done | bytes 589856 | tf_op jit(solution)/shard_map/ppermute | solution.py:49
  146.3 2.2 collective-permute-start.55
  148.5 9.8 %collective-permute-done.58 = bf16[4,96,768]{2,1,0:T(8,128)(2,1)S(1)} collective-permute-done((bf16[4,96,768]{2,1,0:T(8,128)(2,1)S(1)}, bf16[4,96,768]{2,1,0:T(8,128)(2,1)S(1)}, u32[]{:S(2)}, u32[]{:S(2)}) %collective-permute-start.58) | collective-permute-done | bytes 589856 | tf_op jit(solution)/shard_map/ppermute | solution.py:49
  158.5 2.2 collective-permute-start.59
  162.1 2.2 collective-permute-done.57
  165.3 2.3 collective-permute-start.34
  168.4 5.3 %collective-permute-start.32 = (bf16[32,1536]{1,0:T(8,128)(2,1)S(1)}, bf16[32,1536]{1,0:T(8,128)(2,1)S(1)}, u32[]{:S(2)}, u32[]{:S(2)}) collective-permute-start(bf16[32,1536]{1,0:T(8,128)(2,1)S(1)} %get-tuple-element.169), channel_id=1, source_target_pairs={{0,8},{4,12},{8,0},{12,4},{16,24},{20,28},{24,16},{28,20},{1,9},{5... | collective-permute-start | bytes 294920 | tf_op jit(solution)/shard_map/ppermute | solution.py:43
  173.7 6.5 %collective-permute-done.60 = bf16[96,768]{1,0:T(8,128)(2,1)S(1)} collective-permute-done((bf16[96,768]{1,0:T(8,128)(2,1)S(1)}, bf16[96,768]{1,0:T(8,128)(2,1)S(1)}, u32[]{:S(2)}, u32[]{:S(2)}) %collective-permute-start.60) | collective-permute-done | bytes 147488 | tf_op jit(solution)/shard_map/ppermute | solution.py:43
  180.3 2.7 collective-permute-done.33
  186.7 1.8 copy.202
  188.6 1.8 copy.203
  190.3 1.7 collective-permute-start.36
  197.4 1.8 convolution_convert_fusion.3
  200.4 2.3 convolution_convert_fusion.5
  204.9 5.9 %attention_backward.1 = (bf16[512,576]{1,0:T(8,128)(2,1)S(1)}, f32[3,1024]{1,0:T(4,128)S(1)}) custom-call(bf16[512,576]{1,0:T(8,128)(2,1)S(1)} %copy-done.1, f32[3,512,512]{2,1,0:T(8,128)S(1)} %get-tuple-element.15.probs_ref, bf16[512,192]{1,0:T(8,128)(2,1)S(1)} %copy.190.grad_ref), custom_call_target="tpu_custom_call" | custom-call | flops 603979776 | bytes 3145728 | tf_op jit(solution)/shard_map/attention_backward/pallas_call | solution.py:173
  218.7 2.0 concatenate.75
  222.8 2.2 convolution_convert_fusion.6
  225.0 9.9 %collective-permute-done.48 = bf16[4,99,192]{1,2,0:T(8,128)(2,1)S(1)} collective-permute-done((bf16[4,99,192]{1,2,0:T(8,128)(2,1)S(1)}, bf16[4,99,192]{1,2,0:T(8,128)(2,1)S(1)}, u32[]{:S(2)}, u32[]{:S(2)}) %collective-permute-start.48) | collective-permute-done | bytes 152096 | tf_op jit(solution)/shard_map/ppermute | solution.py:49
  235.2 2.0 collective-permute-start.51
  237.1 2.5 collective-permute-start.49
  243.7 3.6 %collective-permute-done.43 = bf16[128,768]{1,0:T(8,128)(2,1)S(1)} collective-permute-done((bf16[128,768]{1,0:T(8,128)(2,1)S(1)}, bf16[128,768]{1,0:T(8,128)(2,1)S(1)}, u32[]{:S(2)}, u32[]{:S(2)}) %collective-permute-start.43) | collective-permute-done | bytes 196640 | tf_op jit(solution)/shard_map/ppermute | solution.py:37
  250.7 1.9 collective-permute-start.47
  252.7 2.6 collective-permute-start.45
  255.5 2.2 collective-permute-done.47
  257.7 3.9 %collective-permute-done.46 = bf16[97,576]{1,0:T(8,128)(2,1)S(1)} collective-permute-done((bf16[97,576]{1,0:T(8,128)(2,1)S(1)}, bf16[97,576]{1,0:T(8,128)(2,1)S(1)}, u32[]{:S(2)}, u32[]{:S(2)}) %collective-permute-start.46) | collective-permute-done | bytes 111776 | tf_op jit(solution)/shard_map/ppermute | solution.py:43
  262.9 1.7 collective-permute-start.53
  264.6 2.4 convolution_add_fusion
  (352 shorter events, 74.8 us)
Async XLA Ops:
  7.2 65.9 %all-gather.2.cloned.1.call-start = ((), (), s32[]{:S(2)}) async-start(), calls=%async_computation | async-start | bytes 1548288 | tf_op jit(solution)/shard_map/all_gather | solution.py:255
  7.2 50.1 %collective-permute-start = (bf16[128,768]{1,0:T(8,128)(2,1)}, bf16[128,768]{1,0:T(8,128)(2,1)}, u32[]{:S(2)}, u32[]{:S(2)}) collective-permute-start(bf16[128,768]{1,0:T(8,128)(2,1)} %param.14), channel_id=1, source_target_pairs={{0,2},{1,3},{2,0},{3,1},{4,6},{5,7},{6,4},{7,5},{8,10},{9,11},{10,... | collective-permute-start | bytes 589832 | tf_op jit(solution)/shard_map/ppermute | solution.py:37
  10.3 48.4 %collective-permute-start.2 = (bf16[128,768]{1,0:T(8,128)(2,1)}, bf16[128,768]{1,0:T(8,128)(2,1)}, u32[]{:S(2)}, u32[]{:S(2)}) collective-permute-start(bf16[128,768]{1,0:T(8,128)(2,1)} %param.14), channel_id=1, source_target_pairs={{0,1},{1,0},{2,3},{3,2},{4,5},{5,4},{6,7},{7,6},{8,9},{9,8},{10,11... | collective-permute-start | bytes 589832 | tf_op jit(solution)/shard_map/ppermute | solution.py:37
  17.2 9.8 %collective-permute-start.16 = (bf16[96,768]{1,0:T(8,128)(2,1)S(1)}, bf16[96,768]{1,0:T(8,128)(2,1)S(1)}, u32[]{:S(2)}, u32[]{:S(2)}) collective-permute-start(bf16[96,768]{1,0:T(8,128)(2,1)S(1)} %bitcast.215), channel_id=1, source_target_pairs={{0,24},{4,28},{8,16},{12,20},{16,8},{20,12},{24,0},{28,4},{1,25},{... | collective-permute-start | bytes 442376 | tf_op jit(solution)/shard_map/ppermute | solution.py:43
  20.8 22.2 %collective-permute-start.17 = (bf16[96,768]{1,0:T(8,128)(2,1)S(1)}, bf16[96,768]{1,0:T(8,128)(2,1)S(1)}, u32[]{:S(2)}, u32[]{:S(2)}) collective-permute-start(bf16[96,768]{1,0:T(8,128)(2,1)S(1)} %bitcast.214), channel_id=1, source_target_pairs={{0,16},{4,20},{8,24},{12,28},{16,0},{20,4},{24,8},{28,12},{1,17},{... | collective-permute-start | bytes 442376 | tf_op jit(solution)/shard_map/ppermute | solution.py:43
  21.0 22.1 %collective-permute-start.18 = (bf16[96,768]{1,0:T(8,128)(2,1)S(1)}, bf16[96,768]{1,0:T(8,128)(2,1)S(1)}, u32[]{:S(2)}, u32[]{:S(2)}) collective-permute-start(bf16[96,768]{1,0:T(8,128)(2,1)S(1)} %bitcast.213), channel_id=1, source_target_pairs={{0,8},{4,12},{8,0},{12,4},{16,24},{20,28},{24,16},{28,20},{1,9},{5... | collective-permute-start | bytes 442376 | tf_op jit(solution)/shard_map/ppermute | solution.py:43
  26.9 19.4 %collective-permute-start.12 = (bf16[96,768]{1,0:T(8,128)(2,1)S(1)}, bf16[96,768]{1,0:T(8,128)(2,1)S(1)}, u32[]{:S(2)}, u32[]{:S(2)}) collective-permute-start(bf16[96,768]{1,0:T(8,128)(2,1)S(1)} %bitcast.218), channel_id=1, source_target_pairs={{0,24},{4,28},{8,16},{12,20},{16,8},{20,12},{24,0},{28,4},{1,25},{... | collective-permute-start | bytes 442376 | tf_op jit(solution)/shard_map/ppermute | solution.py:43
  43.1 12.8 %collective-permute-start.13 = (bf16[96,768]{1,0:T(8,128)(2,1)S(1)}, bf16[96,768]{1,0:T(8,128)(2,1)S(1)}, u32[]{:S(2)}, u32[]{:S(2)}) collective-permute-start(bf16[96,768]{1,0:T(8,128)(2,1)S(1)} %bitcast.217), channel_id=1, source_target_pairs={{0,16},{4,20},{8,24},{12,28},{16,0},{20,4},{24,8},{28,12},{1,17},{... | collective-permute-start | bytes 442376 | tf_op jit(solution)/shard_map/ppermute | solution.py:43
  43.1 12.8 %collective-permute-start.14 = (bf16[96,768]{1,0:T(8,128)(2,1)S(1)}, bf16[96,768]{1,0:T(8,128)(2,1)S(1)}, u32[]{:S(2)}, u32[]{:S(2)}) collective-permute-start(bf16[96,768]{1,0:T(8,128)(2,1)S(1)} %bitcast.216), channel_id=1, source_target_pairs={{0,8},{4,12},{8,0},{12,4},{16,24},{20,28},{24,16},{28,20},{1,9},{5... | collective-permute-start | bytes 442376 | tf_op jit(solution)/shard_map/ppermute | solution.py:43
  47.0 12.1 %collective-permute-start.20 = (bf16[128,768]{1,0:T(8,128)(2,1)S(1)}, bf16[128,768]{1,0:T(8,128)(2,1)S(1)}, u32[]{:S(2)}, u32[]{:S(2)}) collective-permute-start(bf16[128,768]{1,0:T(8,128)(2,1)S(1)} %copy-done.33), channel_id=1, source_target_pairs={{0,2},{1,3},{2,0},{3,1},{4,6},{5,7},{6,4},{7,5},{8,10},{9,11},{10,... | collective-permute-start | bytes 589832 | tf_op jit(solution)/shard_map/ppermute | solution.py:37
  55.8 16.1 %collective-permute-start.19 = (bf16[4,96,768]{2,1,0:T(8,128)(2,1)S(1)}, bf16[4,96,768]{2,1,0:T(8,128)(2,1)S(1)}, u32[]{:S(2)}, u32[]{:S(2)}) collective-permute-start(bf16[4,96,768]{2,1,0:T(8,128)(2,1)S(1)} %pad_maximum_fusion.5), channel_id=1, source_target_pairs={{0,4},{4,0},{8,12},{12,8},{16,20},{20,16},{24,28},{28,24},{1,5},{5... | collective-permute-start | bytes 1769480 | tf_op jit(solution)/shard_map/ppermute | solution.py:49
  58.6 29.3 %collective-permute-start.15 = (bf16[4,96,768]{2,1,0:T(8,128)(2,1)}, bf16[4,96,768]{2,1,0:T(8,128)(2,1)}, u32[]{:S(2)}, u32[]{:S(2)}) collective-permute-start(bf16[4,96,768]{2,1,0:T(8,128)(2,1)} %pad_maximum_fusion.4), channel_id=1, source_target_pairs={{0,4},{4,0},{8,12},{12,8},{16,20},{20,16},{24,28},{28,24},{1,5},{5... | collective-permute-start | bytes 1769480 | tf_op jit(solution)/shard_map/ppermute | solution.py:49
  89.9 7.0 %collective-permute-start.5 = (bf16[128,768]{1,0:T(8,128)(2,1)S(1)}, bf16[128,768]{1,0:T(8,128)(2,1)S(1)}, u32[]{:S(2)}, u32[]{:S(2)}) collective-permute-start(bf16[128,768]{1,0:T(8,128)(2,1)S(1)} %add_convert_fusion.5), channel_id=1, source_target_pairs={{0,2},{1,3},{2,0},{3,1},{4,6},{5,7},{6,4},{7,5},{8,10},{9,11},{10,... | collective-permute-start | bytes 589832 | tf_op jit(solution)/shard_map/ppermute | solution.py:37
  97.7 11.3 %collective-permute-start.6 = (bf16[32,768]{1,0:T(8,128)(2,1)S(1)}, bf16[32,768]{1,0:T(8,128)(2,1)S(1)}, u32[]{:S(2)}, u32[]{:S(2)}) collective-permute-start(bf16[32,768]{1,0:T(8,128)(2,1)S(1)} %get-tuple-element.186), channel_id=1, source_target_pairs={{0,8},{4,12},{8,0},{12,4},{16,24},{20,28},{24,16},{28,20},{1,9},{5... | collective-permute-start | bytes 147464 | tf_op jit(solution)/shard_map/ppermute | solution.py:43
  99.3 9.7 %collective-permute-start.7 = (bf16[32,768]{1,0:T(8,128)(2,1)S(1)}, bf16[32,768]{1,0:T(8,128)(2,1)S(1)}, u32[]{:S(2)}, u32[]{:S(2)}) collective-permute-start(bf16[32,768]{1,0:T(8,128)(2,1)S(1)} %get-tuple-element.185), channel_id=1, source_target_pairs={{0,16},{4,20},{8,24},{12,28},{16,0},{20,4},{24,8},{28,12},{1,17},{... | collective-permute-start | bytes 147464 | tf_op jit(solution)/shard_map/ppermute | solution.py:43
  103.3 5.9 %collective-permute-start.8 = (bf16[32,768]{1,0:T(8,128)(2,1)S(1)}, bf16[32,768]{1,0:T(8,128)(2,1)S(1)}, u32[]{:S(2)}, u32[]{:S(2)}) collective-permute-start(bf16[32,768]{1,0:T(8,128)(2,1)S(1)} %get-tuple-element.184), channel_id=1, source_target_pairs={{0,24},{4,28},{8,16},{12,20},{16,8},{20,12},{24,0},{28,4},{1,25},{... | collective-permute-start | bytes 147464 | tf_op jit(solution)/shard_map/ppermute | solution.py:43
  103.3 6.3 %collective-permute-start.23 = (bf16[32,768]{1,0:T(8,128)(2,1)S(1)}, bf16[32,768]{1,0:T(8,128)(2,1)S(1)}, u32[]{:S(2)}, u32[]{:S(2)}) collective-permute-start(bf16[32,768]{1,0:T(8,128)(2,1)S(1)} %get-tuple-element.181), channel_id=1, source_target_pairs={{0,8},{4,12},{8,0},{12,4},{16,24},{20,28},{24,16},{28,20},{1,9},{5... | collective-permute-start | bytes 147464 | tf_op jit(solution)/shard_map/ppermute | solution.py:43
  103.9 6.9 %collective-permute-start.24 = (bf16[32,768]{1,0:T(8,128)(2,1)S(1)}, bf16[32,768]{1,0:T(8,128)(2,1)S(1)}, u32[]{:S(2)}, u32[]{:S(2)}) collective-permute-start(bf16[32,768]{1,0:T(8,128)(2,1)S(1)} %get-tuple-element.180), channel_id=1, source_target_pairs={{0,16},{4,20},{8,24},{12,28},{16,0},{20,4},{24,8},{28,12},{1,17},{... | collective-permute-start | bytes 147464 | tf_op jit(solution)/shard_map/ppermute | solution.py:43
  109.0 6.0 %collective-permute-start.25 = (bf16[32,768]{1,0:T(8,128)(2,1)S(1)}, bf16[32,768]{1,0:T(8,128)(2,1)S(1)}, u32[]{:S(2)}, u32[]{:S(2)}) collective-permute-start(bf16[32,768]{1,0:T(8,128)(2,1)S(1)} %get-tuple-element.179), channel_id=1, source_target_pairs={{0,24},{4,28},{8,16},{12,20},{16,8},{20,12},{24,0},{28,4},{1,25},{... | collective-permute-start | bytes 147464 | tf_op jit(solution)/shard_map/ppermute | solution.py:43
  109.2 13.2 %collective-permute-start.9 = (bf16[128,768]{1,0:T(8,128)(2,1)S(1)}, bf16[128,768]{1,0:T(8,128)(2,1)S(1)}, u32[]{:S(2)}, u32[]{:S(2)}) collective-permute-start(bf16[128,768]{1,0:T(8,128)(2,1)S(1)} %pad_maximum_fusion.7), channel_id=1, source_target_pairs={{0,1},{1,0},{2,3},{3,2},{4,5},{5,4},{6,7},{7,6},{8,9},{9,8},{10,11... | collective-permute-start | bytes 589832 | tf_op jit(solution)/shard_map/ppermute | solution.py:37
  109.3 7.3 %collective-permute-start.10 = (bf16[128,768]{1,0:T(8,128)(2,1)S(1)}, bf16[128,768]{1,0:T(8,128)(2,1)S(1)}, u32[]{:S(2)}, u32[]{:S(2)}) collective-permute-start(bf16[128,768]{1,0:T(8,128)(2,1)S(1)} %pad_maximum_fusion.7), channel_id=1, source_target_pairs={{0,2},{1,3},{2,0},{3,1},{4,6},{5,7},{6,4},{7,5},{8,10},{9,11},{10,... | collective-permute-start | bytes 589832 | tf_op jit(solution)/shard_map/ppermute | solution.py:37
  114.9 7.4 %collective-permute-start.26 = (bf16[128,768]{1,0:T(8,128)(2,1)S(1)}, bf16[128,768]{1,0:T(8,128)(2,1)S(1)}, u32[]{:S(2)}, u32[]{:S(2)}) collective-permute-start(bf16[128,768]{1,0:T(8,128)(2,1)S(1)} %pad_maximum_fusion.8), channel_id=1, source_target_pairs={{0,1},{1,0},{2,3},{3,2},{4,5},{5,4},{6,7},{7,6},{8,9},{9,8},{10,11... | collective-permute-start | bytes 589832 | tf_op jit(solution)/shard_map/ppermute | solution.py:37
  115.0 7.3 %collective-permute-start.27 = (bf16[128,768]{1,0:T(8,128)(2,1)S(1)}, bf16[128,768]{1,0:T(8,128)(2,1)S(1)}, u32[]{:S(2)}, u32[]{:S(2)}) collective-permute-start(bf16[128,768]{1,0:T(8,128)(2,1)S(1)} %pad_maximum_fusion.8), channel_id=1, source_target_pairs={{0,2},{1,3},{2,0},{3,1},{4,6},{5,7},{6,4},{7,5},{8,10},{9,11},{10,... | collective-permute-start | bytes 589832 | tf_op jit(solution)/shard_map/ppermute | solution.py:37
  129.8 35.3 %collective-permute-start.29 = (bf16[128,1536]{1,0:T(8,128)(2,1)S(1)}, bf16[128,1536]{1,0:T(8,128)(2,1)S(1)}, u32[]{:S(2)}, u32[]{:S(2)}) collective-permute-start(bf16[128,1536]{1,0:T(8,128)(2,1)S(1)} %get-tuple-element.117), channel_id=1, source_target_pairs={{0,1},{1,0},{2,3},{3,2},{4,5},{5,4},{6,7},{7,6},{8,9},{9,8},{10,11... | collective-permute-start | bytes 1179656 | tf_op jit(solution)/shard_map/ppermute | solution.py:37
  129.9 16.2 %collective-permute-start.54 = (bf16[4,96,768]{2,1,0:T(8,128)(2,1)S(1)}, bf16[4,96,768]{2,1,0:T(8,128)(2,1)S(1)}, u32[]{:S(2)}, u32[]{:S(2)}) collective-permute-start(bf16[4,96,768]{2,1,0:T(8,128)(2,1)S(1)} %fusion.35), channel_id=1, source_target_pairs={{0,4},{4,0},{8,12},{12,8},{16,20},{20,16},{24,28},{28,24},{1,5},{5... | collective-permute-start | bytes 1769480 | tf_op jit(solution)/shard_map/ppermute | solution.py:49
  132.6 25.7 %collective-permute-start.58 = (bf16[4,96,768]{2,1,0:T(8,128)(2,1)S(1)}, bf16[4,96,768]{2,1,0:T(8,128)(2,1)S(1)}, u32[]{:S(2)}, u32[]{:S(2)}) collective-permute-start(bf16[4,96,768]{2,1,0:T(8,128)(2,1)S(1)} %fusion.36), channel_id=1, source_target_pairs={{0,4},{4,0},{8,12},{12,8},{16,20},{20,16},{24,28},{28,24},{1,5},{5... | collective-permute-start | bytes 1769480 | tf_op jit(solution)/shard_map/ppermute | solution.py:49
  133.3 31.7 %collective-permute-start.31 = (bf16[128,1536]{1,0:T(8,128)(2,1)S(1)}, bf16[128,1536]{1,0:T(8,128)(2,1)S(1)}, u32[]{:S(2)}, u32[]{:S(2)}) collective-permute-start(bf16[128,1536]{1,0:T(8,128)(2,1)S(1)} %add_convert_fusion.1), channel_id=1, source_target_pairs={{0,2},{1,3},{2,0},{3,1},{4,6},{5,7},{6,4},{7,5},{8,10},{9,11},{10,... | collective-permute-start | bytes 1179656 | tf_op jit(solution)/shard_map/ppermute | solution.py:37
  146.3 12.2 %collective-permute-start.55 = (bf16[96,768]{1,0:T(8,128)(2,1)S(1)}, bf16[96,768]{1,0:T(8,128)(2,1)S(1)}, u32[]{:S(2)}, u32[]{:S(2)}) collective-permute-start(bf16[96,768]{1,0:T(8,128)(2,1)S(1)} %get-tuple-element.154), channel_id=1, source_target_pairs={{0,24},{4,28},{8,16},{12,20},{16,8},{20,12},{24,0},{28,4},{1,25},{... | collective-permute-start | bytes 442376 | tf_op jit(solution)/shard_map/ppermute | solution.py:43
  148.5 12.2 %collective-permute-start.56 = (bf16[96,768]{1,0:T(8,128)(2,1)S(1)}, bf16[96,768]{1,0:T(8,128)(2,1)S(1)}, u32[]{:S(2)}, u32[]{:S(2)}) collective-permute-start(bf16[96,768]{1,0:T(8,128)(2,1)S(1)} %get-tuple-element.153), channel_id=1, source_target_pairs={{0,16},{4,20},{8,24},{12,28},{16,0},{20,4},{24,8},{28,12},{1,17},{... | collective-permute-start | bytes 442376 | tf_op jit(solution)/shard_map/ppermute | solution.py:43
  158.3 6.0 %collective-permute-start.57 = (bf16[96,768]{1,0:T(8,128)(2,1)S(1)}, bf16[96,768]{1,0:T(8,128)(2,1)S(1)}, u32[]{:S(2)}, u32[]{:S(2)}) collective-permute-start(bf16[96,768]{1,0:T(8,128)(2,1)S(1)} %get-tuple-element.152), channel_id=1, source_target_pairs={{0,8},{4,12},{8,0},{12,4},{16,24},{20,28},{24,16},{28,20},{1,9},{5... | collective-permute-start | bytes 442376 | tf_op jit(solution)/shard_map/ppermute | solution.py:43
  158.5 9.9 %collective-permute-start.59 = (bf16[96,768]{1,0:T(8,128)(2,1)S(1)}, bf16[96,768]{1,0:T(8,128)(2,1)S(1)}, u32[]{:S(2)}, u32[]{:S(2)}) collective-permute-start(bf16[96,768]{1,0:T(8,128)(2,1)S(1)} %get-tuple-element.151), channel_id=1, source_target_pairs={{0,24},{4,28},{8,16},{12,20},{16,8},{20,12},{24,0},{28,4},{1,25},{... | collective-permute-start | bytes 442376 | tf_op jit(solution)/shard_map/ppermute | solution.py:43
  160.7 19.5 %collective-permute-start.60 = (bf16[96,768]{1,0:T(8,128)(2,1)S(1)}, bf16[96,768]{1,0:T(8,128)(2,1)S(1)}, u32[]{:S(2)}, u32[]{:S(2)}) collective-permute-start(bf16[96,768]{1,0:T(8,128)(2,1)S(1)} %get-tuple-element.150), channel_id=1, source_target_pairs={{0,16},{4,20},{8,24},{12,28},{16,0},{20,4},{24,8},{28,12},{1,17},{... | collective-permute-start | bytes 442376 | tf_op jit(solution)/shard_map/ppermute | solution.py:43
  164.3 16.0 %collective-permute-start.61 = (bf16[96,768]{1,0:T(8,128)(2,1)S(1)}, bf16[96,768]{1,0:T(8,128)(2,1)S(1)}, u32[]{:S(2)}, u32[]{:S(2)}) collective-permute-start(bf16[96,768]{1,0:T(8,128)(2,1)S(1)} %get-tuple-element.149), channel_id=1, source_target_pairs={{0,8},{4,12},{8,0},{12,4},{16,24},{20,28},{24,16},{28,20},{1,9},{5... | collective-permute-start | bytes 442376 | tf_op jit(solution)/shard_map/ppermute | solution.py:43
  165.3 15.1 %collective-permute-start.34 = (bf16[32,1536]{1,0:T(8,128)(2,1)S(1)}, bf16[32,1536]{1,0:T(8,128)(2,1)S(1)}, u32[]{:S(2)}, u32[]{:S(2)}) collective-permute-start(bf16[32,1536]{1,0:T(8,128)(2,1)S(1)} %get-tuple-element.167), channel_id=1, source_target_pairs={{0,24},{4,28},{8,16},{12,20},{16,8},{20,12},{24,0},{28,4},{1,25},{... | collective-permute-start | bytes 294920 | tf_op jit(solution)/shard_map/ppermute | solution.py:43
  167.5 15.6 %collective-permute-start.33 = (bf16[32,1536]{1,0:T(8,128)(2,1)S(1)}, bf16[32,1536]{1,0:T(8,128)(2,1)S(1)}, u32[]{:S(2)}, u32[]{:S(2)}) collective-permute-start(bf16[32,1536]{1,0:T(8,128)(2,1)S(1)} %get-tuple-element.168), channel_id=1, source_target_pairs={{0,16},{4,20},{8,24},{12,28},{16,0},{20,4},{24,8},{28,12},{1,17},{... | collective-permute-start | bytes 294920 | tf_op jit(solution)/shard_map/ppermute | solution.py:43
  168.4 14.7 %collective-permute-start.32 = (bf16[32,1536]{1,0:T(8,128)(2,1)S(1)}, bf16[32,1536]{1,0:T(8,128)(2,1)S(1)}, u32[]{:S(2)}, u32[]{:S(2)}) collective-permute-start(bf16[32,1536]{1,0:T(8,128)(2,1)S(1)} %get-tuple-element.169), channel_id=1, source_target_pairs={{0,8},{4,12},{8,0},{12,4},{16,24},{20,28},{24,16},{28,20},{1,9},{5... | collective-permute-start | bytes 294920 | tf_op jit(solution)/shard_map/ppermute | solution.py:43
  186.3 6.8 %collective-permute-start.39 = (bf16[128,768]{1,0:T(8,128)(2,1)}, bf16[128,768]{1,0:T(8,128)(2,1)}, u32[]{:S(2)}, u32[]{:S(2)}) collective-permute-start(bf16[128,768]{1,0:T(8,128)(2,1)} %add_convert_fusion.3), channel_id=1, source_target_pairs={{0,2},{1,3},{2,0},{3,1},{4,6},{5,7},{6,4},{7,5},{8,10},{9,11},{10,... | collective-permute-start | bytes 589832 | tf_op jit(solution)/shard_map/ppermute | solution.py:37
  190.3 6.5 %collective-permute-start.36 = (bf16[128,768]{1,0:T(8,128)(2,1)}, bf16[128,768]{1,0:T(8,128)(2,1)}, u32[]{:S(2)}, u32[]{:S(2)}) collective-permute-start(bf16[128,768]{1,0:T(8,128)(2,1)} %get-tuple-element.134), channel_id=1, source_target_pairs={{0,2},{1,3},{2,0},{3,1},{4,6},{5,7},{6,4},{7,5},{8,10},{9,11},{10,... | collective-permute-start | bytes 589832 | tf_op jit(solution)/shard_map/ppermute | solution.py:37
  192.1 30.1 %collective-permute-start.35 = (bf16[128,768]{1,0:T(8,128)(2,1)}, bf16[128,768]{1,0:T(8,128)(2,1)}, u32[]{:S(2)}, u32[]{:S(2)}) collective-permute-start(bf16[128,768]{1,0:T(8,128)(2,1)} %get-tuple-element.134), channel_id=1, source_target_pairs={{0,1},{1,0},{2,3},{3,2},{4,5},{5,4},{6,7},{7,6},{8,9},{9,8},{10,11... | collective-permute-start | bytes 589832 | tf_op jit(solution)/shard_map/ppermute | solution.py:37
  196.9 26.0 %collective-permute-start.37 = (bf16[128,768]{1,0:T(8,128)(2,1)}, bf16[128,768]{1,0:T(8,128)(2,1)}, u32[]{:S(2)}, u32[]{:S(2)}) collective-permute-start(bf16[128,768]{1,0:T(8,128)(2,1)} %collective-permute-done.36), channel_id=1, source_target_pairs={{0,1},{1,0},{2,3},{3,2},{4,5},{5,4},{6,7},{7,6},{8,9},{9,8},{10,11... | collective-permute-start | bytes 589832 | tf_op jit(solution)/shard_map/ppermute | solution.py:37
  213.9 23.2 %collective-permute-start.42 = (bf16[128,768]{1,0:T(8,128)(2,1)}, bf16[128,768]{1,0:T(8,128)(2,1)}, u32[]{:S(2)}, u32[]{:S(2)}) collective-permute-start(bf16[128,768]{1,0:T(8,128)(2,1)} %get-tuple-element.132), channel_id=1, source_target_pairs={{0,1},{1,0},{2,3},{3,2},{4,5},{5,4},{6,7},{7,6},{8,9},{9,8},{10,11... | collective-permute-start | bytes 589832 | tf_op jit(solution)/shard_map/ppermute | solution.py:37
  213.9 29.7 %collective-permute-start.41 = (bf16[128,768]{1,0:T(8,128)(2,1)}, bf16[128,768]{1,0:T(8,128)(2,1)}, u32[]{:S(2)}, u32[]{:S(2)}) collective-permute-start(bf16[128,768]{1,0:T(8,128)(2,1)} %get-tuple-element.131), channel_id=1, source_target_pairs={{0,1},{1,0},{2,3},{3,2},{4,5},{5,4},{6,7},{7,6},{8,9},{9,8},{10,11... | collective-permute-start | bytes 589832 | tf_op jit(solution)/shard_map/ppermute | solution.py:37
  217.3 31.1 %collective-permute-start.44 = (bf16[4,97,576]{2,0,1:T(4,128)(2,1)}, bf16[4,97,576]{2,0,1:T(4,128)(2,1)}, u32[]{:S(2)}, u32[]{:S(2)}) collective-permute-start(bf16[4,97,576]{2,0,1:T(4,128)(2,1)} %fusion.40), channel_id=1, source_target_pairs={{0,4},{4,0},{8,12},{12,8},{16,20},{20,16},{24,28},{28,24},{1,5},{5... | collective-permute-start | bytes 1340936 | tf_op jit(solution)/shard_map/ppermute | solution.py:49
  222.2 12.8 %collective-permute-start.48 = (bf16[4,99,192]{1,2,0:T(8,128)(2,1)S(1)}, bf16[4,99,192]{1,2,0:T(8,128)(2,1)S(1)}, u32[]{:S(2)}, u32[]{:S(2)}) collective-permute-start(bf16[4,99,192]{1,2,0:T(8,128)(2,1)S(1)} %fusion.62), channel_id=1, source_target_pairs={{0,4},{4,0},{8,12},{12,8},{16,20},{20,16},{24,28},{28,24},{1,5},{5... | collective-permute-start | bytes 456200 | tf_op jit(solution)/shard_map/ppermute | solution.py:49
  235.2 6.4 %collective-permute-start.51 = (bf16[99,192]{0,1:T(8,128)(2,1)S(1)}, bf16[99,192]{0,1:T(8,128)(2,1)S(1)}, u32[]{:S(2)}, u32[]{:S(2)}) collective-permute-start(bf16[99,192]{0,1:T(8,128)(2,1)S(1)} %get-tuple-element.175), channel_id=1, source_target_pairs={{0,24},{4,28},{8,16},{12,20},{16,8},{20,12},{24,0},{28,4},{1,25},{... | collective-permute-start | bytes 114056 | tf_op jit(solution)/shard_map/ppermute | solution.py:43
  250.7 7.0 %collective-permute-start.47 = (bf16[97,576]{1,0:T(8,128)(2,1)S(1)}, bf16[97,576]{1,0:T(8,128)(2,1)S(1)}, u32[]{:S(2)}, u32[]{:S(2)}) collective-permute-start(bf16[97,576]{1,0:T(8,128)(2,1)S(1)} %bitcast.219), channel_id=1, source_target_pairs={{0,24},{4,28},{8,16},{12,20},{16,8},{20,12},{24,0},{28,4},{1,25},{... | collective-permute-start | bytes 335240 | tf_op jit(solution)/shard_map/ppermute | solution.py:43
  252.6 9.0 %collective-permute-start.46 = (bf16[97,576]{1,0:T(8,128)(2,1)S(1)}, bf16[97,576]{1,0:T(8,128)(2,1)S(1)}, u32[]{:S(2)}, u32[]{:S(2)}) collective-permute-start(bf16[97,576]{1,0:T(8,128)(2,1)S(1)} %bitcast.220), channel_id=1, source_target_pairs={{0,16},{4,20},{8,24},{12,28},{16,0},{20,4},{24,8},{28,12},{1,17},{... | collective-permute-start | bytes 335240 | tf_op jit(solution)/shard_map/ppermute | solution.py:43
  252.7 8.9 %collective-permute-start.45 = (bf16[97,576]{1,0:T(8,128)(2,1)S(1)}, bf16[97,576]{1,0:T(8,128)(2,1)S(1)}, u32[]{:S(2)}, u32[]{:S(2)}) collective-permute-start(bf16[97,576]{1,0:T(8,128)(2,1)S(1)} %bitcast.221), channel_id=1, source_target_pairs={{0,8},{4,12},{8,0},{12,4},{16,24},{20,28},{24,16},{28,20},{1,9},{5... | collective-permute-start | bytes 335240 | tf_op jit(solution)/shard_map/ppermute | solution.py:43
  (69 other events, 454.3 us)
Sparse Core Ops, SparseCore 0:
  14.7 50.7 all-gather.1
